TPU v7x, 256 devices: a whole 4x4x8 slice. The times are simulated.
256 devices in a mesh: ctx: 64 (over z, y, core), head: 4 (over x).
Axes of the slice: x: 4, y: 4, z: 8, core: 2. Of those that a mesh axis runs over, the one named last changes fastest.
Arguments:
- query_act: bfloat16 [16384, 4096], P('ctx', 'head'), may hold values from -6 to 6
- key_act: bfloat16 [16384, 4096], P('ctx', 'head'), may hold values from -6 to 6
- value_act: bfloat16 [16384, 4096], P('ctx', 'head'), may hold values from -6 to 6
- out_weight: bfloat16 [3072, 4096], P('ctx', 'head'), may hold values from -0.09375 to 0.09375
- out_cotangent: bfloat16 [16384, 3072], P('ctx', 'head'), may hold values from -16 to 16
Outputs:
- grad_query: bfloat16 [16384, 4096], P('ctx', 'head')
- grad_key: bfloat16 [16384, 4096], P('ctx', 'head')
- grad_value: bfloat16 [16384, 4096], P('ctx', 'head')
- grad_weight: float32 [3072, 4096], P('ctx', 'head')
All inputs are finite; a program needn't handle non-finite values.
Results may differ from a plain program's by a relative error of at most 0.014.
Values may be sent and summed in bfloat16 or wider, within the bound.
A program may use at most 128 MiB of HBM per device.

v0:
```python
import math

import jax
import jax.numpy as jnp
from jax import lax
from jax.sharding import Mesh
from jax.sharding import PartitionSpec as P

HDIM = 128
BLK = 256
CTX = ("ctx_0", "ctx_1", "ctx_2")


EPS = 1e-06


def copy_for_each(x, axis):
    copies = jnp.broadcast_to(x, (lax.axis_size(axis), *x.shape))
    return lax.all_to_all(copies, axis, split_axis=0, concat_axis=0, tiled=True)


def in_order(pieces, dim):
    lengths = list(pieces.shape[1:])
    lengths[dim] *= pieces.shape[0]
    return jnp.moveaxis(pieces, 0, dim).reshape(lengths)


def gathered_copies(x, axis, dim):
    pieces = copy_for_each(x, axis)
    return in_order(pieces, dim)


def gather_in_order(x, axes, turns):
    pieces = x[None]
    for k in turns:
        pieces = lax.all_gather(pieces, axes[k], axis=0, tiled=True)
    current = [lax.axis_size(axes[k]) for k in reversed(turns)]
    pieces = pieces.reshape(*current, *x.shape)
    turned = sorted(range(len(turns)), key=lambda place: turns[len(turns) - 1 - place])
    return pieces.transpose(*turned, *range(len(turns), pieces.ndim)).reshape(-1, *x.shape)


def gathered_by_axis(x, axes, turns, dim):
    return in_order(gather_in_order(x, axes, turns), dim)


def filled_with(x, identity):
    return jnp.broadcast_to(jnp.asarray(identity, x.dtype), x.shape)


def entering(x, axes, combine, identity):
    before = start = filled_with(x, identity)
    so_far = x
    for axis in reversed(axes):
        peers, mine = (lax.axis_size(axis), lax.axis_index(axis))
        pieces = lax.all_gather(so_far, axis)
        inside, so_far = (start, start)
        for k in range(peers):
            passed = k < mine
            so_far = combine(so_far, pieces[k])
            inside = jnp.where(passed, so_far, inside)
        before = combine(inside, before)
    return before


def entering_2(x, axes, combine, identity):
    before = start = filled_with(x, identity)
    so_far = x
    for axis in reversed(axes):
        peers, mine = (lax.axis_size(axis), lax.axis_index(axis))
        pieces = lax.all_gather(so_far.astype(jnp.bfloat16), axis)
        inside, so_far = (start, start)
        for k in reversed(range(peers)):
            passed = k > mine
            so_far = combine(so_far, pieces[k].astype(x.dtype))
            inside = jnp.where(passed, so_far, inside)
        before = combine(inside, before)
    return before


def plus(earlier, later_part):
    return earlier + later_part


def body(query_act, key_act, value_act, out_weight, out_cotangent):
    tok_rows = query_act.shape[0]
    width = query_act.shape[1]
    heads = width // HDIM
    nb = tok_rows // BLK
    ctx_count = lax.axis_size(CTX)
    scale = 1.0 / math.sqrt(tok_rows * ctx_count)
    cot_full = gathered_copies(out_cotangent, "head", 1)
    columns = cot_full
    d_attn = jnp.dot(
        columns, gathered_by_axis(out_weight, CTX, (1, 0, 2), 0), preferred_element_type=jnp.float32
    )
    shape4 = (nb, BLK, heads, HDIM)
    q4 = query_act.reshape(shape4)
    k4 = key_act.reshape(shape4)
    v4 = value_act.reshape(shape4)
    block_kv = jnp.einsum("bthi,bthj->bhij", k4, v4, preferred_element_type=jnp.float32)
    shard_kv = jnp.sum(block_kv, axis=0)
    zeros_state = jnp.zeros_like(shard_kv)
    incoming = entering(shard_kv, CTX, plus, zeros_state)
    prior = (incoming[None] + jnp.cumsum(block_kv, axis=0) - block_kv).astype(jnp.bfloat16)
    mask = jnp.tril(jnp.ones((BLK, BLK), jnp.float32))
    scores = (
        jnp.einsum("bthi,bshi->bhts", q4, k4, preferred_element_type=jnp.float32) * mask
    ).astype(jnp.bfloat16)
    raw = jnp.einsum("bhts,bshj->bthj", scores, v4, preferred_element_type=jnp.float32)
    raw = raw + jnp.einsum("bthi,bhij->bthj", q4, prior, preferred_element_type=jnp.float32)
    inv_rms = lax.rsqrt(jnp.mean(raw * raw, axis=-1, keepdims=True) + EPS)
    normal = raw * inv_rms
    normed = normal.astype(jnp.bfloat16).reshape(tok_rows, width)
    d_in = d_attn.reshape(shape4)
    center = jnp.mean(d_in * normal, axis=-1, keepdims=True)
    d_raw = (inv_rms * (d_in - normal * center)).astype(jnp.bfloat16)
    block_g = jnp.einsum("bthi,bthj->bhij", q4, d_raw, preferred_element_type=jnp.float32)
    shard_g = jnp.sum(block_g, axis=0)
    incoming_g = entering_2(shard_g, CTX, plus, zeros_state)
    later = (incoming_g[None] + shard_g[None] - jnp.cumsum(block_g, axis=0)).astype(jnp.bfloat16)
    d_scores = (
        jnp.einsum("bthj,bshj->bhts", d_raw, v4, preferred_element_type=jnp.float32) * mask
    ).astype(jnp.bfloat16)
    grad_q = jnp.einsum("bhts,bshi->bthi", d_scores, k4, preferred_element_type=jnp.float32)
    grad_q = grad_q + jnp.einsum(
        "bthj,bhij->bthi", d_raw, prior, preferred_element_type=jnp.float32
    )
    grad_k = jnp.einsum("bhts,bthi->bshi", d_scores, q4, preferred_element_type=jnp.float32)
    grad_k = grad_k + jnp.einsum("bshj,bhij->bshi", v4, later, preferred_element_type=jnp.float32)
    grad_v = jnp.einsum("bhts,bthj->bshj", scores, d_raw, preferred_element_type=jnp.float32)
    grad_v = grad_v + jnp.einsum("bshi,bhij->bshj", k4, later, preferred_element_type=jnp.float32)
    contract = (((0,), (0,)), ((), ()))
    columns = cot_full
    grad_weight = lax.psum_scatter(
        lax.dot_general(columns, normed, contract, preferred_element_type=jnp.float32) * scale,
        CTX,
        scatter_dimension=0,
        tiled=True,
    )
    return (
        grad_q.reshape(tok_rows, width).astype(jnp.bfloat16),
        grad_k.reshape(tok_rows, width).astype(jnp.bfloat16),
        grad_v.reshape(tok_rows, width).astype(jnp.bfloat16),
        grad_weight,
    )


def solution(mesh):
    finer = Mesh(
        mesh.devices.reshape(8, 4, 2, mesh.shape["head"]), ("ctx_0", "ctx_1", "ctx_2", "head")
    )
    in_specs = (P(CTX, "head"), P(CTX, "head"), P(CTX, "head"), P(CTX, "head"), P(CTX, "head"))
    out_specs = (P(CTX, "head"), P(CTX, "head"), P(CTX, "head"), P(CTX, "head"))
    return jax.shard_map(body, mesh=finer, in_specs=in_specs, out_specs=out_specs, check_vma=False)
```

profile of v0, /device:TPU:1, one launch (start us, length us, event | category | flops | bytes accessed | tf_op | source)
XLA Modules:
  0.0 456.1 jit_solution(10114107526568177707)
XLA Ops:
  7.2 1.2 copy.111
  8.5 0.3 copy.79
  8.8 1.1 fusion.24
  10.0 19.3 %all-gather.22.cloned.1.call-done = f32[16,128,128]{2,1,0:T(8,128)} async-done(((f32[8,128,128]{2,1,0:T(8,128)}), f32[16,128,128]{2,1,0:T(8,128)}) %all-gather.22.cloned.1.call-update) | async-done | bytes 1048592 | tf_op jit(solution)/shard_map/all_gather | solution.py:56
  29.3 2.0 slice_add_fusion.10
  31.5 10.6 %all-gather.1 = bf16[192,1024]{1,0:T(8,128)(2,1)} all-gather(bf16[48,1024]{1,0:T(8,128)(2,1)S(1)} %copy-done.23), channel_id=3, replica_groups=mesh['ctx_0'=8,'ctx_1'=4,'ctx_2'=2,'head'=4] {'ctx_1'}, dimensions={0}, use_global_device_ids=true | all-gather | bytes 491520 | tf_op jit(solution)/shard_map/all_gather | solution.py:36
  42.1 23.6 %all-gather.24.cloned.1.call-done = f32[32,128,128]{2,1,0:T(8,128)} async-done(((f32[8,128,128]{2,1,0:T(8,128)}), f32[32,128,128]{2,1,0:T(8,128)}) %all-gather.24.cloned.1.call-update) | async-done | bytes 2097168 | tf_op jit(solution)/shard_map/all_gather | solution.py:56
  65.7 2.4 fusion.35
  68.2 44.1 %all-gather.14.cloned.1.call-done = bf16[32,48,1024]{2,1,0:T(8,128)(2,1)} async-done(((bf16[4,48,1024]{2,1,0:T(8,128)(2,1)}), bf16[32,48,1024]{2,1,0:T(8,128)(2,1)}) %all-gather.14.cloned.1.call-update) | async-done | bytes 3145744 | tf_op jit(solution)/shard_map/all_gather | solution.py:36
  112.4 1.2 broadcast_in_dim.26
  113.6 4.1 all-to-all-start
  117.8 0.4 multiply_convert_fusion.1
  118.2 1.0 copy-done.1
  119.2 1.5 convolution_bitcast_fusion.3
  120.6 16.6 %all-to-all-done = bf16[4,256,768]{2,1,0:T(8,128)(2,1)S(1)} async-done(((bf16[4,256,768]{2,1,0:T(8,128)(2,1)}), bf16[4,256,768]{2,1,0:T(8,128)(2,1)S(1)}, u32[]{:S(2)}, u32[]{:S(2)}) %all-to-all-start) | async-done | bytes 1572896 | tf_op jit(solution)/shard_map/all_to_all | solution.py:19
  137.3 2.4 copy.83
  139.7 4.1 reshape.315
  143.8 24.5 %all-gather.12.cloned.1.call-done = f32[8,8,128,128]{3,2,1,0:T(8,128)} async-done(((f32[1,8,128,128]{3,2,1,0:T(8,128)}), f32[8,8,128,128]{3,2,1,0:T(8,128)}) %all-gather.12.cloned.1.call-update) | async-done | bytes 4194320 | tf_op jit(solution)/shard_map/all_gather | solution.py:56
  168.3 4.0 fusion.19
  172.3 1.3 multiply_reduce_fusion.1
  173.6 17.7 %all-gather.16.cloned.1.call-done = bf16[64,48,1024]{2,1,0:T(8,128)(2,1)} async-done(((bf16[32,48,1024]{2,1,0:T(8,128)(2,1)}), bf16[64,48,1024]{2,1,0:T(8,128)(2,1)}) %all-gather.16.cloned.1.call-update) | async-done | bytes 6291472 | tf_op jit(solution)/shard_map/all_gather | solution.py:36
  191.4 6.7 %copy.84 = bf16[8,4,2,48,1024]{4,3,2,1,0:T(8,128)(2,1)} copy(bf16[8,4,2,48,1024]{4,3,1,0,2:T(8,128)(2,1)} %bitcast.159) | data formatting | bytes 12582912 | tf_op jit(solution)/shard_map/transpose | solution.py:40
  198.1 8.6 %copy.85 = bf16[1024,3072]{1,0:T(8,128)(2,1)} copy(bf16[1024,3072]{0,1:T(8,128)(2,1)} %bitcast.156) | data formatting | bytes 12582912 | tf_op jit(solution)/shard_map/dot_general | solution.py:94
  206.7 5.4 %multiply_reduce_fusion = (f32[256,8]{0,1:T(8,128)S(1)}, f32[1,256,8,128]{1,3,2,0:T(8,128)S(1)}) fusion(f32[1,256,8,128]{1,3,2,0:T(8,128)} %get-tuple-element.23, f32[256,8]{0,1:T(8,128)S(1)} %add_rsqrt_fusion, bf16[256,3072,1]{1,0,2:T(8,128)(2,1)} %reshape.315, bf16[8,128,3072]{2,1,0:T(8,128)(2,1)} %bitcast.160), kind=kOutput, calls=%fused_computation.17 | convolution fusion | flops 1611397120 | bytes 9977856 | tf_op jit(solution)/shard_map/dot_general | solution.py:94
  212.2 1.1 multiply_convert_fusion.3
  213.2 1.1 fusion.51
  214.4 2.2 all-gather.2
  216.5 0.8 copy-done.11
  217.3 0.8 fusion.49
  218.2 26.3 %all-gather.18.cloned.1.call-done = bf16[4,8,128,128]{3,2,1,0:T(8,128)(2,1)} async-done(((bf16[1,8,128,128]{3,2,1,0:T(8,128)(2,1)}), bf16[4,8,128,128]{3,2,1,0:T(8,128)(2,1)}) %all-gather.18.cloned.1.call-update) | async-done | bytes 1048592 | tf_op jit(solution)/shard_map/all_gather | solution.py:71
  244.5 2.0 fusion.37
  247.0 0.8 copy-done.20
  247.8 6.3 %multiply_bitcast_fusion = f32[3072,1024]{0,1:T(8,128)} fusion(bf16[256,1024]{0,1:T(8,128)(2,1)S(1)} %bitcast.163, bf16[256,3072]{1,0:T(8,128)(2,1)S(1)} %bitcast.161), kind=kOutput, calls=%fused_computation | convolution fusion | flops 1613758464 | bytes 14680064 | tf_op jit(solution)/shard_map/dot_general | solution.py:136
  254.2 12.7 %copy.105 = f32[3072,1024]{1,0:T(8,128)} copy(f32[3072,1024]{0,1:T(8,128)} %multiply_bitcast_fusion) | data formatting | bytes 25165824
  266.9 0.5 multiply_convert_fusion
  267.4 0.5 copy-done.7
  267.9 0.5 convolution_bitcast_fusion.2
  268.4 1.1 fusion.1
  269.5 2.1 copy.96
  271.6 1.3 fusion.52
  272.9 1.3 convolution_bitcast_fusion.1
  274.2 11.2 %all-gather.20.cloned.1.call-done = bf16[8,8,128,128]{3,2,1,0:T(8,128)(2,1)} async-done(((bf16[1,8,128,128]{3,2,1,0:T(8,128)(2,1)}), bf16[8,8,128,128]{3,2,1,0:T(8,128)(2,1)}) %all-gather.20.cloned.1.call-update) | async-done | bytes 2097168 | tf_op jit(solution)/shard_map/all_gather | solution.py:71
  285.4 2.4 fusion.38
  287.8 0.3 fusion.2
  288.1 1.0 copy.97
  289.1 0.3 fusion.3
  289.5 1.0 copy.98
  290.5 158.7 %reduce-scatter.4.cloned.1.call-done = f32[48,1024]{1,0:T(8,128)} async-done(((f32[3072,1024]{1,0:T(8,128)}), f32[48,1024]{1,0:T(8,128)}) %reduce-scatter.4.cloned.1.call-update) | async-done | bytes 196624
  (64 shorter events, 1.0 us)
Async XLA Ops:
  7.2 110.6 %copy-start = (bf16[256,1024]{1,0:T(8,128)(2,1)S(1)}, bf16[256,1024]{1,0:T(8,128)(2,1)}, u32[]{:S(2)}) copy-start(bf16[256,1024]{1,0:T(8,128)(2,1)} %param.5) | copy-start | bytes 1572868
  7.2 1.6 copy-start.5
  7.2 22.1 %all-gather.22.cloned.1.call-start = ((), (), s32[]{:S(2)}) async-start(), calls=%async_computation.7 | async-start | bytes 1572864 | tf_op jit(solution)/shard_map/all_gather | solution.py:56
  8.8 22.6 %copy-start.6 = (bf16[256,8,128]{0,2,1:T(8,128)(2,1)}, bf16[256,8,128]{0,2,1:T(8,128)(2,1)S(1)}, u32[]{:S(2)}) copy-start(bf16[256,8,128]{0,2,1:T(8,128)(2,1)S(1)} %copy.79) | copy-start | bytes 1572868
  8.8 22.6 %copy-start.23 = (bf16[48,1024]{1,0:T(8,128)(2,1)S(1)}, bf16[48,1024]{1,0:T(8,128)(2,1)}, u32[]{:S(2)}) copy-start(bf16[48,1024]{1,0:T(8,128)(2,1)} %param.8) | copy-start | bytes 294916
  9.9 55.8 %all-gather.24.cloned.1.call-start = ((), (), s32[]{:S(2)}) async-start(), calls=%async_computation.8 | async-start | bytes 2621440 | tf_op jit(solution)/shard_map/all_gather | solution.py:56
  31.4 80.9 %all-gather.14.cloned.1.call-start = ((), (), s32[]{:S(2)}) async-start(), calls=%async_computation.3 | async-start | bytes 3538944 | tf_op jit(solution)/shard_map/all_gather | solution.py:36
  42.1 126.2 %all-gather.12.cloned.1.call-start = ((), (), s32[]{:S(2)}) async-start(), calls=%async_computation.2 | async-start | bytes 4718592 | tf_op jit(solution)/shard_map/all_gather | solution.py:56
  68.1 44.2 %copy-start.22 = (bf16[256,768]{1,0:T(8,128)(2,1)S(1)}, bf16[256,768]{1,0:T(8,128)(2,1)}, u32[]{:S(2)}) copy-start(bf16[256,768]{1,0:T(8,128)(2,1)} %param.9) | copy-start | bytes 1179652
  68.2 123.2 %all-gather.16.cloned.1.call-start = ((), (), s32[]{:S(2)}) async-start(), calls=%async_computation.4 | async-start | bytes 9437184 | tf_op jit(solution)/shard_map/all_gather | solution.py:36
  113.6 4.1 copy-start.9
  113.6 23.7 %all-to-all-start = ((bf16[4,256,768]{2,1,0:T(8,128)(2,1)}), bf16[4,256,768]{2,1,0:T(8,128)(2,1)S(1)}, u32[]{:S(2)}, u32[]{:S(2)}) async-start(bf16[4,256,768]{2,1,0:T(8,128)(2,1)} %broadcast_in_dim.26), calls=%async_computation | async-start | bytes 3145728 | tf_op jit(solution)/shard_map/all_to_all | solution.py:19
  117.7 126.8 %all-gather.18.cloned.1.call-start = ((), (), s32[]{:S(2)}) async-start(), calls=%async_computation.5 | async-start | bytes 1310720 | tf_op jit(solution)/shard_map/all_gather | solution.py:71
  118.2 1.0 copy-start.1
  139.7 28.6 %copy-start.8 = (f32[8,128,128]{2,1,0:T(8,128)S(1)}, f32[8,128,128]{2,1,0:T(8,128)}, u32[]{:S(2)}) copy-start(f32[8,128,128]{2,1,0:T(8,128)} %fusion.24) | copy-start | bytes 1572868
  168.3 4.0 copy-start.17
  172.3 1.3 copy-start.18
  206.7 5.4 %copy-start.15 = (f32[1,256,8,128]{1,3,2,0:T(8,128)S(1)}, f32[1,256,8,128]{1,3,2,0:T(8,128)}, u32[]{:S(2)}) copy-start(f32[1,256,8,128]{1,3,2,0:T(8,128)} %get-tuple-element.23) | copy-start | bytes 3145732
  216.5 0.8 copy-start.11
  218.1 67.2 %all-gather.20.cloned.1.call-start = ((), (), s32[]{:S(2)}) async-start(), calls=%async_computation.6 | async-start | bytes 2359296 | tf_op jit(solution)/shard_map/all_gather | solution.py:71
  246.6 202.7 %reduce-scatter.4.cloned.1.call-start = ((), (), s32[]{:S(2)}) async-start(), calls=%async_computation.9 | async-start | bytes 12779520
  246.8 1.0 copy-start.20
  266.9 1.0 copy-start.7
  266.9 1.5 copy-start.19
  267.9 1.6 copy-start.3
  268.4 3.1 copy-start.2
  271.6 1.3 copy-start.4
  271.6 13.8 %copy-start.12 = (bf16[16,128,128]{2,1,0:T(8,128)(2,1)S(1)}, bf16[16,128,128]{2,1,0:T(8,128)(2,1)}, u32[]{:S(2)}) copy-start(bf16[16,128,128]{2,1,0:T(8,128)(2,1)} %copy-done.11) | copy-start | bytes 1572868
  272.9 12.5 %copy-start.16 = (bf16[4,8,128,128]{3,2,1,0:T(8,128)(2,1)S(1)}, bf16[4,8,128,128]{3,2,1,0:T(8,128)(2,1)}, u32[]{:S(2)}) copy-start(bf16[4,8,128,128]{3,2,1,0:T(8,128)(2,1)} %all-gather.18.cloned.1.call-done) | copy-start | bytes 3145732
  272.9 12.5 %copy-start.21 = (f32[8,128,128]{2,1,0:T(8,128)S(1)}, f32[8,128,128]{2,1,0:T(8,128)}, u32[]{:S(2)}) copy-start(f32[8,128,128]{2,1,0:T(8,128)} %get-tuple-element.27) | copy-start | bytes 1572868
  285.4 2.4 copy-start.14
  287.8 1.4 copy-start.10
  287.8 1.4 copy-start.13
Sparse Core Ops, SparseCore 0:
  10.4 18.8 all-gather.21
  31.7 33.9 all-gather.23
  67.5 44.7 all-gather.13
  114.5 53.6 all-gather.11
  169.9 21.4 all-gather.15
  218.3 26.1 all-gather.17
  246.7 38.6 all-gather.19
  290.2 158.9 reduce-scatter.3
where the time goes:
time: 460 us; the launch traced here: 456 us
  waiting for transfers between devices  342 us (74%)
  local copies, waits for them, and re-layouts  44.8 us (10%)
  matrix products  22.5 us (5%)
  other arithmetic  14.8 us (3%)
  between operations  14.4 us (3%)
  blocking collectives  12.7 us (3%)
    unnamed x9, waiting for transfers between devices  159 us
    all_gather x3, waiting for transfers between devices, entering(): pieces = lax.all_gather(so_far, axis)  67.4 us
    all_gather x2, waiting for transfers between devices, gather_in_order(): pieces = lax.all_gather(pieces, axes[k], axis=0, tiled=True)  61.8 us
    all_gather x2, waiting for transfers between devices, entering_2(): pieces = lax.all_gather(so_far.astype(jnp.bfloat16), axis)  37.5 us
    unnamed x53, local copies, waits for them, and re-layouts  21.2 us
    all_to_all x1, waiting for transfers between devices, copy_for_each(): return lax.all_to_all(copies, axis, split_axis=0, concat_axis=0, tiled=True)  16.6 us
    all_gather x1, blocking collectives, gather_in_order(): pieces = lax.all_gather(pieces, axes[k], axis=0, tiled=True)  10.6 us
  transfers between devices with their start and end apart: 9, of which 9 were waited for; matrix products, arithmetic and copies ran while one was open for 11% of the time, Pallas kernels for 0%

commit v1 on v0

v1 whole, which is shorter than its diff:
```python
import functools

import jax
import jax.numpy as jnp
from jax import lax
from jax.experimental import pallas as pl
from jax.experimental.pallas import tpu as pltpu
from jax.sharding import Mesh
from jax.sharding import PartitionSpec as P

HDIM = 128
BLK = 256
EPS = 1e-06
NZ, NY, NC, NX = 8, 4, 2, 4
HEADS = 8
ROWS = 48
WIDTH = 1024
COLS = 768
SLAB = NY * NC * ROWS
PA = 16
PB = 32
F32 = jnp.float32
BF16 = jnp.bfloat16
GRADW_SCALE = 1.0 / 128.0


def dot_nn(a, b):
    return lax.dot_general(a, b, (((1,), (0,)), ((), ())), preferred_element_type=F32)


def dot_nt(a, b):
    return lax.dot_general(a, b, (((1,), (1,)), ((), ())), preferred_element_type=F32)


def dot_tn(a, b):
    return lax.dot_general(a, b, (((0,), (0,)), ((), ())), preferred_element_type=F32)


def kernel(
    q_hbm, k_hbm, v_hbm, w_hbm, cot_hbm,
    gq_ref, gk_ref, gv_ref, gw_ref,
    q, k, v, wb, cot, cot_t, cot_t_sib, normed, normed_sib, scores, raw, inv, da, draw, pk, pv,
    part, st1, r1, st2, r2, red, zst, zr, qst, qr, qy1s, qy1r, qy2s, qy2r,
    s_send, a_recv, a_pre, b_tot, b1_recv, b_base, b2_recv, c_send, c_recv,
    load_sem, cx1, cx2, zp_sem, yp1, yp2, qy1, qy2, zq, sib, tsib, nsib,
    ry1, ry2, rz, qz, qya, qyb, sa, sb1, sb2, sc,
):
    z, y, c, x = (lax.axis_index(n) for n in ("z", "y", "c", "x"))
    up_z, dn_z = lax.rem(z + 1, NZ), lax.rem(z + NZ - 1, NZ)
    up_y, dn_y, far_y = lax.rem(y + 1, NY), lax.rem(y + 3, NY), lax.rem(y + 2, NY)
    up_x, dn_x, far_x = lax.rem(x + 1, NX), lax.rem(x + 3, NX), lax.rem(x + 2, NX)
    other = 1 - c
    plane = y * 2 + c
    zdir = ({"z": up_z}, {"z": dn_z})
    ydir = ({"y": up_y}, {"y": dn_y})
    xdir = ({"x": up_x}, {"x": dn_x})
    pending = []

    def send(src, dst, sems, at, device):
        copy = pltpu.make_async_remote_copy(
            src_ref=src, dst_ref=dst, send_sem=sems.at[(0, *at)], recv_sem=sems.at[(1, *at)],
            device_id=device, device_id_type=pl.DeviceIdType.MESH,
        )
        copy.start()
        pending.append(copy)
        return copy

    loads = [
        pltpu.make_async_copy(src, dst, load_sem.at[i])
        for i, (src, dst) in enumerate(
            ((cot_hbm, cot.at[x]), (w_hbm, wb.at[z, y, c]), (k_hbm, k), (v_hbm, v), (q_hbm, q))
        )
    ]
    for load in loads:
        load.start()

    def plane_peer(o):
        j = lax.rem(plane + o, 8)
        return j, {"y": lax.div(j, 2), "c": lax.rem(j, 2)}

    peers = [plane_peer(o)[1] for o in range(1, 8)]
    peers += [{"z": lax.rem(z + o, NZ)} for o in range(1, NZ)]
    peers += list(xdir)
    barrier = pltpu.get_barrier_semaphore()
    for peer in peers:
        pl.semaphore_signal(barrier, inc=1, device_id=peer, device_id_type=pl.DeviceIdType.MESH)
    pl.semaphore_wait(barrier, len(peers))

    loads[0].wait()
    cot1 = [send(cot.at[x], cot.at[x], cx1, (d,), xdir[d]) for d in (0, 1)]
    cot2 = []

    def cot_forward():
        cot1[0].wait_recv()
        half = cot.at[dn_x, pl.ds(0, 128)]
        cot2.append(send(half, half, cx2, (0,), xdir[0]))
        cot1[1].wait_recv()
        half = cot.at[up_x, pl.ds(128, 128)]
        cot2.append(send(half, half, cx2, (1,), xdir[1]))

    ag_z = [lax.rem(z + NZ + o, NZ) for o in (0, -1, 1, -2, 2, -3, 3, 4)]
    zp_c, yp1_c, yp2_c, qy1_c, qy2_c, zq_c, sib_c = {}, {}, {}, {}, {}, {}, {}

    def send_zp(r):
        for d, org in ((0, lax.rem(z + NZ - r, NZ)), (1, lax.rem(z + r, NZ))):
            rows = pl.ds(0, PB) if r < 3 else pl.ds(PA * d, PA)
            blk = wb.at[org, y, c, rows]
            zp_c[d, r] = send(blk, blk, zp_sem, (d, r), zdir[d])

    def send_yp1(i):
        for d in (0, 1):
            blk = wb.at[ag_z[i], y, c, pl.ds(0, PB)]
            yp1_c[d, i] = send(blk, blk, yp1, (d, i), ydir[d])

    def forward_yp(i):
        for d, org in ((0, dn_y), (1, up_y)):
            yp1_c[d, i].wait_recv()
            blk = wb.at[ag_z[i], org, c, pl.ds(PA * d, PA)]
            yp2_c[d, i] = send(blk, blk, yp2, (d, i), ydir[d])

    def send_qy1():
        for d in (0, 1):
            blk = wb.at[z, y, c, pl.ds(PB, PA)]
            qy1_c[d] = send(blk, blk, qy1, (d,), ydir[d])

    def forward_qy():
        for d, org in ((0, dn_y), (1, up_y)):
            qy1_c[d].wait_recv()
            blk = wb.at[z, org, c, pl.ds(PB, PA), pl.ds(512 * d, 512)]
            qy2_c[d] = send(blk, blk, qy2, (d,), ydir[d])

    def send_zq(r):
        for d, org in ((0, lax.rem(z + NZ - r, NZ)), (1, lax.rem(z + r, NZ))):
            ys = pl.ds(0, NY) if r < 3 else pl.ds(2 * d, 2)
            blk = wb.at[org, ys, c, pl.ds(PB, PA)]
            zq_c[d, r] = send(blk, blk, zq, (d, r), zdir[d])

    def recv_both(copies, r):
        for d in (0, 1):
            copies[d, r].wait_recv()

    def send_sib(i):
        recv_both(yp2_c, i)
        blk = wb.at[ag_z[i], :, c]
        sib_c[i] = send(blk, blk, sib, (i,), {"c": other})

    def ag0():
        send_zp(0)
        send_qy1()
        send_yp1(0)

    def ag1():
        recv_both(zp_c, 0)
        send_zp(1)
        send_yp1(1)
        send_yp1(2)
        forward_qy()
        forward_yp(0)
        qy2_c[0].wait_recv()
        qy2_c[1].wait_recv()
        send_zq(0)

    def ag2():
        recv_both(zp_c, 1)
        send_zp(2)
        send_yp1(3)
        send_yp1(4)
        recv_both(zq_c, 0)
        send_zq(1)
        forward_yp(1)
        forward_yp(2)
        send_sib(0)

    def ag3():
        recv_both(zp_c, 2)
        send_zp(3)
        send_yp1(5)
        send_yp1(6)
        recv_both(zq_c, 1)
        send_zq(2)
        forward_yp(3)
        forward_yp(4)
        send_sib(1)
        send_sib(2)

    def ag4():
        recv_both(zp_c, 3)
        send_yp1(7)
        recv_both(zq_c, 2)
        send_zq(3)
        forward_yp(5)
        forward_yp(6)
        send_sib(3)
        send_sib(4)

    def ag5():
        forward_yp(7)
        send_sib(5)
        send_sib(6)
        recv_both(zq_c, 3)
        send_sib(7)

    class Scan:
        def __init__(self, s):
            self.s = s
            self.order = (range(8), range(7, -1, -1))[s]

        def start(self):
            s = self.s
            self.a = []
            for o in range(1, 8):
                j, dev = plane_peer(o)
                self.a.append(send(s_send.at[s, j], a_recv.at[s, plane], sa, (s, o), dev))
            a_recv[s, plane] = s_send[s, plane]

        def a_done(self):
            s = self.s
            for copy in self.a:
                copy.wait_recv()
            run = jnp.zeros((HDIM, HDIM), F32)
            for j in self.order:
                a_pre[s, j] = run
                run = run + a_recv[s, j].astype(F32)
            b_tot[s] = run.reshape(NZ, 16, HDIM)
            self.b1 = []
            for o in range(1, NZ):
                t = lax.rem(z + o, NZ)
                self.b1.append(send(b_tot.at[s, t], b1_recv.at[s, z], sb1, (s, o), {"z": t}))
            b1_recv[s, z] = b_tot[s, z]

        def b1_done(self):
            s = self.s
            for copy in self.b1:
                copy.wait_recv()
            run = jnp.zeros((16, HDIM), F32)
            for t in self.order:
                b_base[s, t] = run
                run = run + b1_recv[s, t]
            self.b2 = []
            for o in range(1, NZ):
                t = lax.rem(z + o, NZ)
                self.b2.append(send(b_base.at[s, t], b2_recv.at[s, z], sb2, (s, o), {"z": t}))
            b2_recv[s, z] = b_base[s, z]

        def b2_done(self):
            s = self.s
            for copy in self.b2:
                copy.wait_recv()
            base = b2_recv[s].reshape(HDIM, HDIM)
            for j in range(8):
                c_send[s, j] = (base + a_pre[s, j]).astype(BF16)
            self.c = []
            for o in range(1, 8):
                j, dev = plane_peer(o)
                self.c.append(send(c_send.at[s, j], c_recv.at[s, plane], sc, (s, o), dev))
            c_recv[s, plane] = c_send[s, plane]

        def c_done(self):
            for copy in self.c:
                copy.wait_recv()

    kv_scan, g_scan = Scan(0), Scan(1)

    def cols_of(h):
        return pl.ds(pl.multiple_of(h * HDIM, HDIM), HDIM)

    def for_heads(first, count, fn, unroll=2):
        @pl.loop(0, count // unroll)
        def _(i):
            for u in range(unroll):
                fn(first + i * unroll + u)

    mask = (
        lax.broadcasted_iota(jnp.int32, (BLK, BLK), 0)
        >= lax.broadcasted_iota(jnp.int32, (BLK, BLK), 1)
    )

    def kv_head(h):
        cs = cols_of(h)
        s_send[0, h] = dot_tn(k[:, cs], v[:, cs]).astype(BF16)

    def score_head(h):
        cs = cols_of(h)
        s = jnp.where(mask, dot_nt(q[:, cs], k[:, cs]), 0.0).astype(BF16)
        scores[h] = s
        raw[:, cs] = dot_nn(s, v[:, cs])

    def norm_head(h):
        cs = cols_of(h)
        r = raw[:, cs] + dot_nn(q[:, cs], c_recv[0, h])
        i = lax.rsqrt(jnp.mean(r * r, axis=-1, keepdims=True) + EPS)
        a = r * i
        raw[:, cs] = a
        inv[h] = i
        normed[:, cs] = a.astype(BF16)

    def draw_head(h):
        cs = cols_of(h)
        d, a = da[:, cs], raw[:, cs]
        center = jnp.mean(d * a, axis=-1, keepdims=True)
        dr = (inv[h] * (d - a * center)).astype(BF16)
        draw[:, cs] = dr
        s_send[1, h] = dot_tn(q[:, cs], dr).astype(BF16)

    def local_grad_head(h):
        cs = cols_of(h)
        dr = draw[:, cs]
        ds = jnp.where(mask, dot_nt(dr, v[:, cs]), 0.0).astype(BF16)
        gq_ref[:, cs] = (dot_nn(ds, k[:, cs]) + dot_nt(dr, c_recv[0, h])).astype(BF16)
        pk[:, cs] = dot_tn(ds, q[:, cs])
        pv[:, cs] = dot_tn(scores[h], dr)

    def final_grad_head(h):
        cs = cols_of(h)
        gk_ref[:, cs] = (pk[:, cs] + dot_nt(v[:, cs], c_recv[1, h])).astype(BF16)
        gv_ref[:, cs] = (pv[:, cs] + dot_nn(k[:, cs], c_recv[1, h])).astype(BF16)

    x_order = (x, dn_x, up_x, far_x)
    tsib_c = {}

    def turn(i):
        xo = x_order[i]
        for half in (0, 1):
            t = cot[xo, :, pl.ds(half * SLAB, SLAB)].T
            cot_t[xo * 2 + half] = t.reshape(NY, NC, ROWS, BLK)
        src = cot_t.at[pl.ds(xo * 2, 2), :, other]
        tsib_c[i] = send(src, cot_t_sib.at[pl.ds(xo * 2, 2)], tsib, (i,), {"c": other})

    def d_attn(idx, first=False):
        for i in idx:
            sib_c[i].wait_recv()

        @pl.loop(0, 4)
        def _(n):
            cs = pl.ds(pl.multiple_of(n * 256, 256), 256)
            acc = None if first else da[:, cs]
            for i in idx:
                zo = ag_z[i]
                lanes = pl.ds(pl.multiple_of(lax.rem(zo, 2) * SLAB, 128), SLAB)
                t = dot_nn(cot[lax.div(zo, 2), :, lanes], wb[zo, :, :, :, cs].reshape(SLAB, 256))
                acc = t if acc is None else acc + t
            da[:, cs] = acc

    rs_z = [lax.rem(z + NZ + o, NZ) for o in (4, 3, -3, 2, -2, 1, -1, 0)]
    up_of, dn_of = (0, 1, 3, 5), (0, 2, 4, 6)
    ry1_c, ry2_c, rz_c, qz_c, qya_c, qyb_c = {}, {}, {}, {}, {}, {}

    def product(i):
        zt = rs_z[i]

        @pl.loop(0, 4)
        def _(n):
            cs = pl.ds(pl.multiple_of(n * 256, 256), 256)
            acc = dot_nn(cot_t[zt, :, c].reshape(NY * ROWS, BLK), normed[:, cs])
            acc = acc + dot_nn(cot_t_sib[zt].reshape(NY * ROWS, BLK), normed_sib[:, cs])
            part[zt, :, :, cs] = acc.reshape(NY, ROWS, 256)

    def step1(i):
        st1[i] = part[rs_z[i], far_y, 0:PB].astype(BF16)
        for d in (0, 1):
            ry1_c[d, i] = send(st1.at[i, pl.ds(PA * d, PA)], r1.at[d, i], ry1, (d, i), ydir[d])

    def step2(i):
        zt = rs_z[i]
        for d, t in ((0, up_y), (1, dn_y)):
            ry1_c[d, i].wait_recv()
            mine, rest = slice(PA * d, PA * d + PA), slice(PA - PA * d, PB - PA * d)
            st2[d, i, mine] = (part[zt, t, mine] + r1[d, i].astype(F32)).astype(BF16)
            st2[d, i, rest] = part[zt, t, rest].astype(BF16)
            ry2_c[d, i] = send(st2.at[d, i], r2.at[d, i], ry2, (d, i), ydir[d])

    def step3(i):
        recv_both(ry2_c, i)
        red[i] = part[rs_z[i], y, 0:PB] + (r2[0, i].astype(F32) + r2[1, i].astype(F32))

    def chain(s):
        for d, idx in ((0, up_of), (1, dn_of)):
            i = idx[s]
            mine = slice(PA * d, PA * d + PA)
            if s == 0:
                zst[d, 0, mine] = red[i, mine].astype(BF16)
                blk = pl.ds(PA * d, PA)
                rz_c[d, s] = send(zst.at[d, 0, blk], zr.at[d, 0, blk], rz, (d, s), zdir[d])
                continue
            rz_c[d, s - 1].wait_recv()
            if s == 1:
                rest = slice(PA - PA * d, PB - PA * d)
                zst[d, s, mine] = (red[i, mine] + zr[d, 0, mine].astype(F32)).astype(BF16)
                zst[d, s, rest] = red[i, rest].astype(BF16)
            else:
                zst[d, s] = (red[i] + zr[d, s - 1].astype(F32)).astype(BF16)
            rz_c[d, s] = send(zst.at[d, s], zr.at[d, s], rz, (d, s), zdir[d])

    def chain_end():
        recv_both(rz_c, 3)
        total = red[7] + (zr[0, 3].astype(F32) + zr[1, 3].astype(F32))
        gw_ref[0:PB] = total * GRADW_SCALE

    def qchain(s):
        for d, idx in ((0, up_of), (1, dn_of)):
            zt = rs_z[idx[s]]
            mine = slice(2 * d, 2 * d + 2)
            if s == 0:
                qst[d, 0, mine] = part[zt, mine, PB:ROWS].astype(BF16)
                blk = pl.ds(2 * d, 2)
                qz_c[d, s] = send(qst.at[d, 0, blk], qr.at[d, 0, blk], qz, (d, s), zdir[d])
                continue
            qz_c[d, s - 1].wait_recv()
            if s == 1:
                rest = slice(2 - 2 * d, 4 - 2 * d)
                got = qr[d, 0, mine].astype(F32)
                qst[d, s, mine] = (part[zt, mine, PB:ROWS] + got).astype(BF16)
                qst[d, s, rest] = part[zt, rest, PB:ROWS].astype(BF16)
            else:
                got = qr[d, s - 1].astype(F32)
                qst[d, s] = (part[zt, :, PB:ROWS] + got).astype(BF16)
            qz_c[d, s] = send(qst.at[d, s], qr.at[d, s], qz, (d, s), zdir[d])

    def q_y1():
        recv_both(qz_c, 3)
        part[z, :, PB:ROWS] = part[z, :, PB:ROWS] + (qr[0, 3].astype(F32) + qr[1, 3].astype(F32))
        for d in (0, 1):
            qy1s[d] = part[z, far_y, PB:ROWS, 512 * d : 512 * d + 512].astype(BF16)
            qya_c[d] = send(qy1s.at[d], qy1r.at[d], qya, (d,), ydir[d])

    def q_y2():
        for d, t in ((0, up_y), (1, dn_y)):
            qya_c[d].wait_recv()
            mine = slice(512 * d, 512 * d + 512)
            rest = slice(512 - 512 * d, 1024 - 512 * d)
            qy2s[d, :, mine] = (part[z, t, PB:ROWS, mine] + qy1r[d].astype(F32)).astype(BF16)
            qy2s[d, :, rest] = part[z, t, PB:ROWS, rest].astype(BF16)
            qyb_c[d] = send(qy2s.at[d], qy2r.at[d], qyb, (d,), ydir[d])

    def q_end():
        for d in (0, 1):
            qyb_c[d].wait_recv()
        total = part[z, y, PB:ROWS] + (qy2r[0].astype(F32) + qy2r[1].astype(F32))
        gw_ref[PB:ROWS] = total * GRADW_SCALE

    loads[1].wait()
    ag0()
    loads[2].wait()
    loads[3].wait()
    for_heads(0, 8, kv_head, 4)
    kv_scan.start()
    loads[4].wait()
    ag1()
    for_heads(0, 4, score_head)
    kv_scan.a_done()
    ag2()
    for_heads(4, 4, score_head)
    kv_scan.b1_done()
    turn(0)
    cot_forward()
    ag3()
    kv_scan.b2_done()
    turn(1)
    turn(2)
    ag4()
    kv_scan.c_done()
    for_heads(0, 8, norm_head)
    nsib_c = send(normed, normed_sib, nsib, (), {"c": other})
    for copy in cot2:
        copy.wait_recv()
    turn(3)
    ag5()
    d_attn((0, 1, 2), True)
    nsib_c.wait_recv()
    for i in range(4):
        tsib_c[i].wait_recv()
    for i in range(8):
        product(i)
        step1(i)
        if i == 0:
            qchain(0)
    d_attn((3, 4))
    d_attn((5, 6))
    qchain(1)
    d_attn((7,))
    for_heads(0, 8, draw_head)
    g_scan.start()
    for i in range(3):
        step2(i)
    qchain(2)
    g_scan.a_done()
    for i in range(3, 7):
        step2(i)
    step3(0)
    chain(0)
    for_heads(0, 4, local_grad_head)
    g_scan.b1_done()
    qchain(3)
    step2(7)
    step3(1)
    step3(2)
    chain(1)
    for_heads(4, 4, local_grad_head)
    g_scan.b2_done()
    step3(3)
    step3(4)
    chain(2)
    q_y1()
    g_scan.c_done()
    for_heads(0, 8, final_grad_head)
    step3(5)
    step3(6)
    chain(3)
    q_y2()
    step3(7)
    q_end()
    chain_end()
    for copy in pending:
        copy.wait_send()


def body(query_act, key_act, value_act, out_weight, out_cotangent):
    vm = pltpu.VMEM
    dma = pltpu.SemaphoreType.DMA
    scratch = [
        vm((BLK, WIDTH), BF16), vm((BLK, WIDTH), BF16), vm((BLK, WIDTH), BF16),
        vm((NZ, NY, NC, ROWS, WIDTH), BF16),
        vm((NX, BLK, COLS), BF16),
        vm((NZ, NY, NC, ROWS, BLK), BF16),
        vm((NZ, NY, ROWS, BLK), BF16),
        vm((BLK, WIDTH), BF16), vm((BLK, WIDTH), BF16),
        vm((HEADS, BLK, BLK), BF16),
        vm((BLK, WIDTH), F32),
        vm((HEADS, BLK, 1), F32),
        vm((BLK, WIDTH), F32),
        vm((BLK, WIDTH), BF16),
        vm((BLK, WIDTH), F32), vm((BLK, WIDTH), F32),
        vm((NZ, NY, ROWS, WIDTH), F32),
        vm((8, PB, WIDTH), BF16), vm((2, 8, PA, WIDTH), BF16),
        vm((2, 8, PB, WIDTH), BF16), vm((2, 8, PB, WIDTH), BF16),
        vm((8, PB, WIDTH), F32),
        vm((2, 4, PB, WIDTH), BF16), vm((2, 4, PB, WIDTH), BF16),
        vm((2, 4, NY, PA, WIDTH), BF16), vm((2, 4, NY, PA, WIDTH), BF16),
        vm((2, PA, 512), BF16), vm((2, PA, 512), BF16),
        vm((2, PA, WIDTH), BF16), vm((2, PA, WIDTH), BF16),
        vm((2, 8, HDIM, HDIM), BF16), vm((2, 8, HDIM, HDIM), BF16),
        vm((2, 8, HDIM, HDIM), F32),
        vm((2, NZ, 16, HDIM), F32), vm((2, NZ, 16, HDIM), F32),
        vm((2, NZ, 16, HDIM), F32), vm((2, NZ, 16, HDIM), F32),
        vm((2, 8, HDIM, HDIM), BF16), vm((2, 8, HDIM, HDIM), BF16),
        dma((5,)), dma((2, 2)), dma((2, 2)),
        dma((2, 2, 4)), dma((2, 2, 8)), dma((2, 2, 8)),
        dma((2, 2)), dma((2, 2)), dma((2, 2, 4)),
        dma((2, 8)), dma((2, 4)), dma((2,)),
        dma((2, 2, 8)), dma((2, 2, 8)), dma((2, 2, 4)), dma((2, 2, 4)),
        dma((2, 2)), dma((2, 2)),
        dma((2, 2, 8)), dma((2, 2, 8)), dma((2, 2, 8)), dma((2, 2, 8)),
    ]
    grad = jax.ShapeDtypeStruct((BLK, WIDTH), BF16)
    return pl.pallas_call(
        kernel,
        out_shape=(grad, grad, grad, jax.ShapeDtypeStruct((ROWS, WIDTH), F32)),
        in_specs=[pl.BlockSpec(memory_space=pl.ANY)] * 5,
        out_specs=[pl.BlockSpec(memory_space=pltpu.VMEM)] * 4,
        scratch_shapes=scratch,
        compiler_params=pltpu.CompilerParams(
            collective_id=0, has_side_effects=True, vmem_limit_bytes=56 * 1024 * 1024
        ),
        name="layer_backward",
    )(query_act, key_act, value_act, out_weight, out_cotangent)


def solution(mesh):
    finer = Mesh(mesh.devices.reshape(NZ, NY, NC, NX), ("z", "y", "c", "x"))
    spec = P(("z", "y", "c"), "x")
    return jax.shard_map(
        body, mesh=finer, in_specs=(spec,) * 5, out_specs=(spec,) * 4, check_vma=False
    )
```

time: 460 us -> 92.7 us (0.20)
  waiting for transfers between devices: 342 us -> 0 us
  Pallas kernels: 0 us -> 86.9 us
  local copies, waits for them, and re-layouts: 44.8 us -> 4.95 us
  matrix products: 22.5 us -> 0 us
  other arithmetic: 14.8 us -> 0 us
  between operations: 14.4 us -> 0.65 us
  blocking collectives: 12.7 us -> 0 us
    all_gather x7 -> x0, waiting for transfers between devices: 167 us -> none  [the longest x3 67.4 us: entering(): pieces = lax.all_gather(so_far, axis)]
    unnamed x9 -> x0, waiting for transfers between devices: 159 us -> none
    pallas_call x0 -> x1, Pallas kernels: none -> 86.9 us  [body(): pl.pallas_call(kernel, out_shape=(grad, grad, grad, jax.ShapeDtypeStruct(...]
    dot_general x14 -> x0, matrix products: 22.5 us -> none  [the longest x1 6.33 us: body(): lax.dot_general(columns, normed, contract, preferred_element_type=jnp.flo...]
    all_to_all x1 -> x0, waiting for transfers between devices: 16.6 us -> none  [copy_for_each(): return lax.all_to_all(copies, axis, split_axis=0, concat_axis=0, tiled=True)]
    unnamed x53 -> x10, local copies, waits for them, and re-layouts: 21.2 us -> 4.95 us
    all_gather x2 -> x0, blocking collectives: 12.7 us -> none  [the longest x1 10.6 us: gather_in_order(): pieces = lax.all_gather(pieces, axes[k], axis=0, tiled=True)]
    convert_element_type x5 -> x0, other arithmetic: 10.3 us -> none  [the longest x1 4.04 us: body(): (incoming[None] + jnp.cumsum(block_kv, axis=0) - block_kv).astype(jnp.bfl...]
  transfers between devices with their start and end apart: 9 -> 0, of which waited for: 9 -> 0; matrix products, arithmetic and copies ran while one was open for 11% -> 0% of each run, Pallas kernels for 0% -> 0%
where the time goes in v1:
time: 92.7 us; the launch traced here: 92.5 us
  Pallas kernels  86.9 us (94%)
  local copies, waits for them, and re-layouts  4.95 us (5%)
    pallas_call x1, Pallas kernels, body(): pl.pallas_call(kernel, out_shape=(grad, grad, grad, jax.ShapeDtypeStruct(...  86.9 us
    unnamed x10, local copies, waits for them, and re-layouts  4.95 us

profile of v1, /device:TPU:1, one launch (start us, length us, event | category | flops | bytes accessed | tf_op | source)
XLA Modules:
  0.0 92.5 jit_solution(18205510572404406774)
XLA Ops:
  0.6 86.9 %layer_backward.1 = (bf16[256,1024]{1,0:T(8,128)(2,1)}, bf16[256,1024]{1,0:T(8,128)(2,1)}, bf16[256,1024]{1,0:T(8,128)(2,1)}, f32[48,1024]{1,0:T(8,128)}) custom-call(bf16[256,1024]{1,0:T(8,128)(2,1)} %q_hbm.1, bf16[256,1024]{1,0:T(8,128)(2,1)} %k_hbm.1, bf16[256,1024]{1,0:T(8,128)(2,1)} %v_hbm.1, bf16[48,1024]{1,0:T(8,128)(2,1)} %w_hbm.1, ...), custom_call_target="tpu_custom_call" | custom-call | tf_op jit(solution)/shard_map/layer_backward/pallas_call | solution.py:555
  87.5 0.0 copy-start.1
  87.5 1.9 %copy.13 = bf16[256,1024]{1,0:T(8,128)(2,1)} copy(bf16[256,1024]{1,0:T(8,128)(2,1)} %get-tuple-element.8) | data formatting | bytes 1048576
  89.4 0.0 copy-done.1
  89.4 0.0 copy-start
  89.4 0.8 copy.14
  90.2 0.4 copy-done
  90.7 0.0 copy-start.2
  90.7 0.8 copy.15
  91.5 0.3 copy-done.2
  91.8 0.7 copy.16
Async XLA Ops:
  87.5 1.9 %copy-start.1 = (bf16[256,1024]{1,0:T(8,128)(2,1)S(1)}, bf16[256,1024]{1,0:T(8,128)(2,1)}, u32[]{:S(2)}) copy-start(bf16[256,1024]{1,0:T(8,128)(2,1)} %get-tuple-element.9) | copy-start | bytes 1572868
  89.4 1.2 %copy-start = (bf16[256,1024]{1,0:T(8,128)(2,1)S(1)}, bf16[256,1024]{1,0:T(8,128)(2,1)}, u32[]{:S(2)}) copy-start(bf16[256,1024]{1,0:T(8,128)(2,1)} %get-tuple-element.10) | copy-start | bytes 1572868
  90.7 1.1 %copy-start.2 = (f32[48,1024]{1,0:T(8,128)S(1)}, f32[48,1024]{1,0:T(8,128)}, u32[]{:S(2)}) copy-start(f32[48,1024]{1,0:T(8,128)} %get-tuple-element.11) | copy-start | bytes 589828

commit v2 on v1

v2 whole, which is shorter than its diff:
```python
import functools

import jax
import jax.numpy as jnp
from jax import lax
from jax.experimental import pallas as pl
from jax.experimental.pallas import tpu as pltpu
from jax.sharding import Mesh
from jax.sharding import PartitionSpec as P

HDIM = 128
BLK = 256
EPS = 1e-06
NZ, NY, NC, NX = 8, 4, 2, 4
HEADS = 8
ROWS = 48
WIDTH = 1024
COLS = 768
SLAB = NY * NC * ROWS
PA = 16
PB = 32
F32 = jnp.float32
BF16 = jnp.bfloat16
GRADW_SCALE = 1.0 / 128.0


def dot_nn(a, b):
    return lax.dot_general(a, b, (((1,), (0,)), ((), ())), preferred_element_type=F32)


def dot_nt(a, b):
    return lax.dot_general(a, b, (((1,), (1,)), ((), ())), preferred_element_type=F32)


def dot_tn(a, b):
    return lax.dot_general(a, b, (((0,), (0,)), ((), ())), preferred_element_type=F32)


def kernel(
    q_hbm, k_hbm, v_hbm, w_hbm, cot_hbm,
    gq_hbm, gk_hbm, gv_hbm, gw_hbm,
    q, k, v, wb, cot, cot_t, cot_o, normed, scores, raw, inv, da, draw, pk, pv, gq, gk, gv, gw,
    part, st1, r1, st2, r2, red, zst, zr, qst, qr, qy1s, qy1r, qy2s, qy2r,
    own, s_send, s_recv, a_send, a_recv, a_pre, b_tot, b1_recv, b_base, b2_recv,
    c_send, c_recv, e_send, e_recv,
    load_sem, store_sem, cx1, cx2, zp_sem, yp1, yp2, qy1, qy2, zq, sib, tsib, nsib,
    ry1, ry2, rz, qz, qya, qyb, ss, sa, sb1, sb2, sc, se,
):
    z, y, c, x = (lax.axis_index(n) for n in ("z", "y", "c", "x"))
    up_z, dn_z = lax.rem(z + 1, NZ), lax.rem(z + NZ - 1, NZ)
    up_y, dn_y, far_y = lax.rem(y + 1, NY), lax.rem(y + 3, NY), lax.rem(y + 2, NY)
    up_x, dn_x, far_x = lax.rem(x + 1, NX), lax.rem(x + 3, NX), lax.rem(x + 2, NX)
    other = 1 - c
    zdir = ({"z": up_z}, {"z": dn_z})
    ydir = ({"y": up_y}, {"y": dn_y})
    xdir = ({"x": up_x}, {"x": dn_x})
    pending = []

    def send(src, dst, sems, at, device):
        copy = pltpu.make_async_remote_copy(
            src_ref=src, dst_ref=dst, send_sem=sems.at[(0, *at)], recv_sem=sems.at[(1, *at)],
            device_id=device, device_id_type=pl.DeviceIdType.MESH,
        )
        copy.start()
        pending.append(copy)
        return copy

    loads = [
        pltpu.make_async_copy(src, dst, load_sem.at[i])
        for i, (src, dst) in enumerate(
            ((cot_hbm, cot.at[x]), (w_hbm, wb.at[z, y, c]), (k_hbm, k), (v_hbm, v), (q_hbm, q))
        )
    ]
    for load in loads:
        load.start()

    peers = [{"c": other}]
    peers += [{"y": lax.rem(y + o, NY)} for o in range(1, NY)]
    peers += [{"z": lax.rem(z + o, NZ)} for o in range(1, NZ)]
    peers += list(xdir)
    barrier = pltpu.get_barrier_semaphore()
    for peer in peers:
        pl.semaphore_signal(barrier, inc=1, device_id=peer, device_id_type=pl.DeviceIdType.MESH)
    pl.semaphore_wait(barrier, len(peers))

    loads[0].wait()
    cot1 = [send(cot.at[x], cot.at[x], cx1, (d,), xdir[d]) for d in (0, 1)]
    cot2 = []

    def cot_forward():
        cot1[0].wait_recv()
        half = cot.at[dn_x, pl.ds(0, 128)]
        cot2.append(send(half, half, cx2, (0,), xdir[0]))
        cot1[1].wait_recv()
        half = cot.at[up_x, pl.ds(128, 128)]
        cot2.append(send(half, half, cx2, (1,), xdir[1]))

    ag_z = [lax.rem(z + NZ + o, NZ) for o in (0, -1, 1, -2, 2, -3, 3, 4)]
    zp_c, yp1_c, yp2_c, qy1_c, qy2_c, zq_c, sib_c = {}, {}, {}, {}, {}, {}, {}

    def send_zp(r):
        for d, org in ((0, lax.rem(z + NZ - r, NZ)), (1, lax.rem(z + r, NZ))):
            rows = pl.ds(0, PB) if r < 3 else pl.ds(PA * d, PA)
            blk = wb.at[org, y, c, rows]
            zp_c[d, r] = send(blk, blk, zp_sem, (d, r), zdir[d])

    def send_yp1(i):
        for d in (0, 1):
            blk = wb.at[ag_z[i], y, c, pl.ds(0, PB)]
            yp1_c[d, i] = send(blk, blk, yp1, (d, i), ydir[d])

    def forward_yp(i):
        for d, org in ((0, dn_y), (1, up_y)):
            yp1_c[d, i].wait_recv()
            blk = wb.at[ag_z[i], org, c, pl.ds(PA * d, PA)]
            yp2_c[d, i] = send(blk, blk, yp2, (d, i), ydir[d])

    def send_qy1():
        for d in (0, 1):
            blk = wb.at[z, y, c, pl.ds(PB, PA)]
            qy1_c[d] = send(blk, blk, qy1, (d,), ydir[d])

    def forward_qy():
        for d, org in ((0, dn_y), (1, up_y)):
            qy1_c[d].wait_recv()
            blk = wb.at[z, org, c, pl.ds(PB, PA), pl.ds(512 * d, 512)]
            qy2_c[d] = send(blk, blk, qy2, (d,), ydir[d])

    q_rows = (y, dn_y, up_y, far_y)

    def send_zq(b, r):
        if r > 0:
            for d in (0, 1):
                zq_c[b, d, r - 1].wait_recv()
        for d, org in ((0, lax.rem(z + NZ - r, NZ)), (1, lax.rem(z + r, NZ))):
            lanes = pl.ds(0, WIDTH) if r < 3 else pl.ds(512 * d, 512)
            blk = wb.at[org, q_rows[b], c, pl.ds(PB, PA), lanes]
            zq_c[b, d, r] = send(blk, blk, zq, (b, d, r), zdir[d])

    def recv_both(copies, r):
        for d in (0, 1):
            copies[d, r].wait_recv()

    def ag_start():
        send_zp(0)
        send_qy1()
        send_zq(0, 0)
        send_yp1(0)

    def ag_q1():
        forward_qy()
        send_zq(1, 0)
        send_zq(2, 0)

    def ag_q2():
        qy2_c[0].wait_recv()
        qy2_c[1].wait_recv()
        send_zq(3, 0)

    def ag_p(r):
        recv_both(zp_c, r - 1)
        if r < 4:
            send_zp(r)
            send_yp1(2 * r - 1)
            send_yp1(2 * r)
        else:
            send_yp1(7)

    def send_sib(i):
        recv_both(yp2_c, i)
        if i == 7:
            for b in range(4):
                zq_c[b, 0, 3].wait_recv()
                zq_c[b, 1, 3].wait_recv()
        blk = wb.at[ag_z[i], :, c]
        sib_c[i] = send(blk, blk, sib, (i,), {"c": other})

    order = (range(8), range(7, -1, -1))
    y_order = (range(NY), range(NY - 1, -1, -1))
    s_c, a_c, b1_c, b2_c, c_c, e_c = {}, {}, {}, {}, {}, {}
    mine4, rest4 = pl.ds(c * 4, 4), pl.ds(other * 4, 4)

    def scan_start(s):
        s_send[s] = own[s, rest4].astype(BF16)
        s_c[s] = send(s_send.at[s], s_recv.at[s], ss, (s,), {"c": other})

    def scan_a(s):
        s_c[s].wait_recv()
        total = own[s, mine4] + s_recv[s].astype(F32)
        a_send[s] = total.astype(BF16)
        for o in range(1, NY):
            t = lax.rem(y + o, NY)
            a_c[s, o] = send(a_send.at[s, t], a_recv.at[s, y], sa, (s, o), {"y": t})
        a_recv[s, y] = a_send[s, y]

    def scan_b1(s):
        for o in range(1, NY):
            a_c[s, o].wait_recv()
        run = jnp.zeros((HDIM, HDIM), F32)
        for t in y_order[s]:
            a_pre[s, t] = run
            run = run + a_recv[s, t].astype(F32)
        b_tot[s] = run.reshape(NZ, 16, HDIM)
        for o in range(1, NZ):
            t = lax.rem(z + o, NZ)
            b1_c[s, o] = send(b_tot.at[s, t], b1_recv.at[s, z], sb1, (s, o), {"z": t})
        b1_recv[s, z] = b_tot[s, z]

    def scan_b2(s):
        for o in range(1, NZ):
            b1_c[s, o].wait_recv()
        run = jnp.zeros((16, HDIM), F32)
        for t in order[s]:
            b_base[s, t] = run
            run = run + b1_recv[s, t]
        for o in range(1, NZ):
            t = lax.rem(z + o, NZ)
            b2_c[s, o] = send(b_base.at[s, t], b2_recv.at[s, z], sb2, (s, o), {"z": t})
        b2_recv[s, z] = b_base[s, z]

    def scan_c(s):
        for o in range(1, NZ):
            b2_c[s, o].wait_recv()
        base = b2_recv[s].reshape(HDIM, HDIM)
        for t in range(NY):
            c_send[s, t] = (base + a_pre[s, t]).astype(BF16)
        for o in range(1, NY):
            t = lax.rem(y + o, NY)
            c_c[s, o] = send(c_send.at[s, t], c_recv.at[s, y], sc, (s, o), {"y": t})
        c_recv[s, y] = c_send[s, y]

    def scan_e(s):
        for o in range(1, NY):
            c_c[s, o].wait_recv()
        first = c == s
        outer = c_recv[s].astype(F32)
        after_own = outer + own[s, mine4]
        after_sib = outer + s_recv[s].astype(F32)
        e_send[s] = jnp.where(first, after_own, outer).astype(BF16)
        e_c[s] = send(e_send.at[s], e_recv.at[s, mine4], se, (s,), {"c": other})
        e_recv[s, mine4] = jnp.where(first, outer, after_sib).astype(BF16)

    def scan_end(s):
        e_c[s].wait_recv()

    def cols_of(h):
        return pl.ds(pl.multiple_of(h * HDIM, HDIM), HDIM)

    def for_heads(first, count, fn, unroll=2):
        @pl.loop(0, count // unroll)
        def _(i):
            for u in range(unroll):
                fn(first + i * unroll + u)

    mask = (
        lax.broadcasted_iota(jnp.int32, (BLK, BLK), 0)
        >= lax.broadcasted_iota(jnp.int32, (BLK, BLK), 1)
    )

    def kv_head(h):
        cs = cols_of(h)
        own[0, h] = dot_tn(k[:, cs], v[:, cs])

    def score_head(h):
        cs = cols_of(h)
        s = jnp.where(mask, dot_nt(q[:, cs], k[:, cs]), 0.0).astype(BF16)
        scores[h] = s
        raw[:, cs] = dot_nn(s, v[:, cs])

    def norm_head(h):
        cs = cols_of(h)
        r = raw[:, cs] + dot_nn(q[:, cs], e_recv[0, h])
        i = lax.rsqrt(jnp.mean(r * r, axis=-1, keepdims=True) + EPS)
        a = r * i
        raw[:, cs] = a
        inv[h] = i
        normed[0:BLK, cs] = a.astype(BF16)

    def draw_head(h):
        cs = cols_of(h)
        d, a = da[:, cs], raw[:, cs]
        center = jnp.mean(d * a, axis=-1, keepdims=True)
        dr = (inv[h] * (d - a * center)).astype(BF16)
        draw[:, cs] = dr
        own[1, h] = dot_tn(q[:, cs], dr)

    def local_grad_head(h):
        cs = cols_of(h)
        dr = draw[:, cs]
        ds = jnp.where(mask, dot_nt(dr, v[:, cs]), 0.0).astype(BF16)
        gq[:, cs] = (dot_nn(ds, k[:, cs]) + dot_nt(dr, e_recv[0, h])).astype(BF16)
        pk[:, cs] = dot_tn(ds, q[:, cs])
        pv[:, cs] = dot_tn(scores[h], dr)

    def final_grad_head(h):
        cs = cols_of(h)
        gk[:, cs] = (pk[:, cs] + dot_nt(v[:, cs], e_recv[1, h])).astype(BF16)
        gv[:, cs] = (pv[:, cs] + dot_nn(k[:, cs], e_recv[1, h])).astype(BF16)

    x_order = (x, dn_x, up_x, far_x)
    tsib_c = {}

    def turn(i):
        xo = x_order[i]
        for half in (0, 1):
            far_first = lax.rem(xo * 2 + half - z + NZ, NZ)
            zi = jnp.where(far_first < 4, 7 - 2 * far_first, 2 * far_first - 8)
            t = cot[xo, :, pl.ds(half * SLAB, SLAB)].T.reshape(NY, NC, ROWS, BLK)
            for yt in range(NY):
                dy = lax.rem(yt - y + NY, NY)
                yi = jnp.where(dy == 0, 3, jnp.where(dy == 2, 0, jnp.where(dy == 1, 1, 2)))
                keep = jnp.where(c == 0, t[yt, 0], t[yt, 1])
                give = jnp.where(c == 0, t[yt, 1], t[yt, 0])
                cot_t[zi, yi, :, 0:BLK] = keep
                cot_o[zi, yi] = give
            tsib_c[i, half] = send(
                cot_o.at[zi], cot_t.at[zi, :, :, pl.ds(BLK, BLK)], tsib, (i, half), {"c": other}
            )

    def d_attn(idx, first=False):
        for i in idx:
            sib_c[i].wait_recv()

        @pl.loop(0, 4)
        def _(n):
            cs = pl.ds(pl.multiple_of(n * 256, 256), 256)
            lhs, rhs = [], []
            for i in idx:
                zo = ag_z[i]
                lanes = pl.ds(pl.multiple_of(lax.rem(zo, 2) * SLAB, 128), SLAB)
                lhs.append(cot[lax.div(zo, 2), :, lanes])
                rhs.append(wb[zo, :, :, :, cs].reshape(SLAB, 256))
            t = dot_nn(jnp.concatenate(lhs, 1), jnp.concatenate(rhs, 0))
            da[:, cs] = t if first else da[:, cs] + t

    up_of, dn_of = (0, 1, 3, 5), (0, 2, 4, 6)
    y_of = (1, 2)
    ry1_c, ry2_c, rz_c, qz_c, qya_c, qyb_c = {}, {}, {}, {}, {}, {}

    def product(lo, hi):
        n = hi - lo

        @pl.loop(0, 4)
        def _(col):
            cs = pl.ds(pl.multiple_of(col * 256, 256), 256)
            acc = dot_nn(cot_t[lo:hi].reshape(n * NY * ROWS, 2 * BLK), normed[:, cs])
            part[lo:hi, :, :, cs] = acc.reshape(n, NY, ROWS, 256)

    def step1(i):
        st1[i] = part[i, 0, 0:PB].astype(BF16)
        for d in (0, 1):
            ry1_c[d, i] = send(st1.at[i, pl.ds(PA * d, PA)], r1.at[d, i], ry1, (d, i), ydir[d])

    def step2(i):
        for d in (0, 1):
            t = y_of[d]
            ry1_c[d, i].wait_recv()
            mine, rest = slice(PA * d, PA * d + PA), slice(PA - PA * d, PB - PA * d)
            st2[d, i, mine] = (part[i, t, mine] + r1[d, i].astype(F32)).astype(BF16)
            st2[d, i, rest] = part[i, t, rest].astype(BF16)
            ry2_c[d, i] = send(st2.at[d, i], r2.at[d, i], ry2, (d, i), ydir[d])

    def step3(i):
        recv_both(ry2_c, i)
        red[i] = part[i, 3, 0:PB] + (r2[0, i].astype(F32) + r2[1, i].astype(F32))

    def chain(s):
        for d, idx in ((0, up_of), (1, dn_of)):
            i = idx[s]
            mine = slice(PA * d, PA * d + PA)
            if s == 0:
                zst[d, 0, mine] = red[i, mine].astype(BF16)
                blk = pl.ds(PA * d, PA)
                rz_c[d, s] = send(zst.at[d, 0, blk], zr.at[d, 0, blk], rz, (d, s), zdir[d])
                continue
            rz_c[d, s - 1].wait_recv()
            if s == 1:
                rest = slice(PA - PA * d, PB - PA * d)
                zst[d, s, mine] = (red[i, mine] + zr[d, 0, mine].astype(F32)).astype(BF16)
                zst[d, s, rest] = red[i, rest].astype(BF16)
            else:
                zst[d, s] = (red[i] + zr[d, s - 1].astype(F32)).astype(BF16)
            rz_c[d, s] = send(zst.at[d, s], zr.at[d, s], rz, (d, s), zdir[d])

    def chain_end():
        recv_both(rz_c, 3)
        total = red[7] + (zr[0, 3].astype(F32) + zr[1, 3].astype(F32))
        gw[0:PB] = total * GRADW_SCALE

    def qchain(b, s):
        ys = pl.ds(2 * b, 2)
        for d, idx in ((0, up_of), (1, dn_of)):
            i = idx[s]
            term = part[i, 2 * b : 2 * b + 2, PB:ROWS]
            if s > 0:
                qz_c[b, d, s - 1].wait_recv()
            if s == 0:
                t = 2 * b + d
                qst[d, 0, t] = part[i, t, PB:ROWS].astype(BF16)
                blk = pl.ds(t, 1)
                qz_c[b, d, s] = send(qst.at[d, 0, blk], qr.at[d, 0, blk], qz, (b, d, s), zdir[d])
                continue
            if s == 1:
                t, u = 2 * b + d, 2 * b + 1 - d
                qst[d, s, t] = (part[i, t, PB:ROWS] + qr[d, 0, t].astype(F32)).astype(BF16)
                qst[d, s, u] = part[i, u, PB:ROWS].astype(BF16)
            else:
                got = qr[d, s - 1, 2 * b : 2 * b + 2].astype(F32)
                qst[d, s, 2 * b : 2 * b + 2] = (term + got).astype(BF16)
            qz_c[b, d, s] = send(qst.at[d, s, ys], qr.at[d, s, ys], qz, (b, d, s), zdir[d])

    def q_sum(b):
        for d in (0, 1):
            qz_c[b, d, 3].wait_recv()
        ys = slice(2 * b, 2 * b + 2)
        got = qr[0, 3, ys].astype(F32) + qr[1, 3, ys].astype(F32)
        part[7, ys, PB:ROWS] = part[7, ys, PB:ROWS] + got

    def q_y1():
        q_sum(0)
        for d in (0, 1):
            qy1s[d] = part[7, 0, PB:ROWS, 512 * d : 512 * d + 512].astype(BF16)
            qya_c[d] = send(qy1s.at[d], qy1r.at[d], qya, (d,), ydir[d])

    def q_y2():
        q_sum(1)
        for d in (0, 1):
            t = y_of[d]
            qya_c[d].wait_recv()
            mine = slice(512 * d, 512 * d + 512)
            rest = slice(512 - 512 * d, 1024 - 512 * d)
            qy2s[d, :, mine] = (part[7, t, PB:ROWS, mine] + qy1r[d].astype(F32)).astype(BF16)
            qy2s[d, :, rest] = part[7, t, PB:ROWS, rest].astype(BF16)
            qyb_c[d] = send(qy2s.at[d], qy2r.at[d], qyb, (d,), ydir[d])

    def q_end():
        for d in (0, 1):
            qyb_c[d].wait_recv()
        total = part[7, 3, PB:ROWS] + (qy2r[0].astype(F32) + qy2r[1].astype(F32))
        gw[PB:ROWS] = total * GRADW_SCALE

    stores = []

    def store(i, src_ref, dst_ref):
        copy = pltpu.make_async_copy(src_ref, dst_ref, store_sem.at[i])
        copy.start()
        stores.append(copy)

    half8 = ((0, 4), (4, 4))
    nsib_c = []

    def kv():
        loads[2].wait()
        loads[3].wait()
        for_heads(0, 8, kv_head, 4)

    def score(n):
        if n == 0:
            loads[4].wait()
        for_heads(*half8[n], score_head, 4)

    def norm(n):
        for_heads(*half8[n], norm_head, 4)
        blk = pl.ds(512 * n, 512)
        src, dst = normed.at[pl.ds(0, BLK), blk], normed.at[pl.ds(BLK, BLK), blk]
        nsib_c.append(send(src, dst, nsib, (n,), {"c": other}))

    def cot_wait():
        for copy in cot2:
            copy.wait_recv()

    def sib_wait():
        for copy in nsib_c:
            copy.wait_recv()
        for copy in tsib_c.values():
            copy.wait_recv()

    def local_grad(n):
        for_heads(*half8[n], local_grad_head, 4)
        if n == 1:
            store(0, gq, gq_hbm)

    def final_grad():
        for_heads(0, 8, final_grad_head, 4)
        store(1, gk, gk_hbm)
        store(2, gv, gv_hbm)

    loads[1].wait()
    ag_start()
    kv()
    scan_start(0)
    score(0)
    score(1)
    scan_a(0)
    ag_q1()
    forward_yp(0)
    ag_p(1)
    send_zq(0, 1)
    turn(0)
    send_zq(1, 1)
    ag_q2()
    send_zq(2, 1)
    scan_b1(0)
    send_sib(0)
    ag_p(2)
    cot_forward()
    forward_yp(1)
    send_zq(0, 2)
    turn(1)
    forward_yp(2)
    send_zq(1, 2)
    send_zq(3, 1)
    turn(2)
    send_zq(2, 2)
    forward_yp(3)
    scan_b2(0)
    forward_yp(4)
    ag_p(3)
    send_zq(0, 3)
    send_sib(1)
    send_sib(2)
    send_zq(1, 3)
    cot_wait()
    turn(3)
    send_zq(3, 2)
    send_zq(2, 3)
    send_sib(3)
    send_sib(4)
    d_attn((0, 1, 2), True)
    scan_c(0)
    forward_yp(5)
    forward_yp(6)
    ag_p(4)
    send_zq(3, 3)
    d_attn((3, 4))
    send_sib(5)
    scan_e(0)
    send_sib(6)
    forward_yp(7)
    scan_end(0)
    norm(0)
    norm(1)
    d_attn((5, 6))
    send_sib(7)
    sib_wait()
    product(0, 1)
    qchain(0, 0)
    qchain(1, 0)
    step1(0)
    product(1, 3)
    d_attn((7,))
    for_heads(0, 8, draw_head, 4)
    scan_start(1)
    qchain(0, 1)
    qchain(1, 1)
    step2(0)
    step1(1)
    step1(2)
    scan_a(1)
    product(3, 5)
    step1(3)
    step1(4)
    product(5, 8)
    step3(0)
    chain(0)
    qchain(0, 2)
    qchain(1, 2)
    step2(1)
    step2(2)
    step1(5)
    step1(6)
    step1(7)
    local_grad(0)
    scan_b1(1)
    step2(3)
    step2(4)
    qchain(0, 3)
    step3(1)
    local_grad(1)
    step3(2)
    chain(1)
    qchain(1, 3)
    step2(5)
    step2(6)
    step2(7)
    scan_b2(1)
    q_y1()
    step3(3)
    step3(4)
    chain(2)
    step3(5)
    step3(6)
    scan_c(1)
    chain(3)
    step3(7)
    q_y2()
    chain_end()
    q_end()
    scan_e(1)
    scan_end(1)
    final_grad()
    store(3, gw, gw_hbm)
    for copy in stores:
        copy.wait()
    for copy in pending:
        copy.wait_send()


def handed_out(*refs):
    ins, outs, held, sems = refs[:4], refs[4:8], refs[8:12], refs[12]
    into = [pltpu.make_async_copy(a, b, sems.at[0, i]) for i, (a, b) in enumerate(zip(ins, held))]
    back = [pltpu.make_async_copy(a, b, sems.at[1, i]) for i, (a, b) in enumerate(zip(held, outs))]
    for copy in into:
        copy.start()
    for i in range(4):
        into[i].wait()
        back[i].start()
    for copy in back:
        copy.wait()


def body(query_act, key_act, value_act, out_weight, out_cotangent):
    vm = pltpu.VMEM
    dma = pltpu.SemaphoreType.DMA
    state = (HDIM, HDIM)
    scratch = [
        vm((BLK, WIDTH), BF16), vm((BLK, WIDTH), BF16), vm((BLK, WIDTH), BF16),
        vm((NZ, NY, NC, ROWS, WIDTH), BF16),
        vm((NX, BLK, COLS), BF16),
        vm((NZ, NY, ROWS, 2 * BLK), BF16), vm((NZ, NY, ROWS, BLK), BF16),
        vm((2 * BLK, WIDTH), BF16),
        vm((HEADS, BLK, BLK), BF16),
        vm((BLK, WIDTH), F32),
        vm((HEADS, BLK, 1), F32),
        vm((BLK, WIDTH), F32),
        vm((BLK, WIDTH), BF16),
        vm((BLK, WIDTH), F32), vm((BLK, WIDTH), F32),
        vm((BLK, WIDTH), BF16), vm((BLK, WIDTH), BF16), vm((BLK, WIDTH), BF16),
        vm((ROWS, WIDTH), F32),
        vm((NZ, NY, ROWS, WIDTH), F32),
        vm((8, PB, WIDTH), BF16), vm((2, 8, PA, WIDTH), BF16),
        vm((2, 8, PB, WIDTH), BF16), vm((2, 8, PB, WIDTH), BF16),
        vm((8, PB, WIDTH), F32),
        vm((2, 4, PB, WIDTH), BF16), vm((2, 4, PB, WIDTH), BF16),
        vm((2, 4, NY, PA, WIDTH), BF16), vm((2, 4, NY, PA, WIDTH), BF16),
        vm((2, PA, 512), BF16), vm((2, PA, 512), BF16),
        vm((2, PA, WIDTH), BF16), vm((2, PA, WIDTH), BF16),
        vm((2, HEADS, *state), F32),
        vm((2, 4, *state), BF16), vm((2, 4, *state), BF16),
        vm((2, 4, *state), BF16), vm((2, 4, *state), BF16), vm((2, 4, *state), F32),
        vm((2, NZ, 16, HDIM), F32), vm((2, NZ, 16, HDIM), F32),
        vm((2, NZ, 16, HDIM), F32), vm((2, NZ, 16, HDIM), F32),
        vm((2, 4, *state), BF16), vm((2, 4, *state), BF16),
        vm((2, 4, *state), BF16), vm((2, HEADS, *state), BF16),
        dma((5,)), dma((4,)), dma((2, 2)), dma((2, 2)),
        dma((2, 2, 4)), dma((2, 2, 8)), dma((2, 2, 8)),
        dma((2, 2)), dma((2, 2)), dma((2, 4, 2, 4)),
        dma((2, 8)), dma((2, 4, 2)), dma((2, 2)),
        dma((2, 2, 8)), dma((2, 2, 8)), dma((2, 2, 4)), dma((2, 2, 2, 4)),
        dma((2, 2)), dma((2, 2)),
        dma((2, 2)), dma((2, 2, 4)), dma((2, 2, 8)), dma((2, 2, 8)), dma((2, 2, 4)), dma((2, 2)),
    ]
    grad = jax.ShapeDtypeStruct((BLK, WIDTH), BF16)
    shapes = (grad, grad, grad, jax.ShapeDtypeStruct((ROWS, WIDTH), F32))
    anywhere = pl.BlockSpec(memory_space=pl.ANY)
    made = pl.pallas_call(
        kernel,
        out_shape=shapes,
        in_specs=[anywhere] * 5,
        out_specs=[anywhere] * 4,
        scratch_shapes=scratch,
        compiler_params=pltpu.CompilerParams(
            collective_id=0, has_side_effects=True, vmem_limit_bytes=56 * 1024 * 1024
        ),
        name="layer_backward",
    )(query_act, key_act, value_act, out_weight, out_cotangent)
    return pl.pallas_call(
        handed_out,
        out_shape=shapes,
        in_specs=[anywhere] * 4,
        out_specs=[anywhere] * 4,
        scratch_shapes=[*(vm(s.shape, s.dtype) for s in shapes), dma((2, 4))],
        name="hand_out",
    )(*made)


def solution(mesh):
    finer = Mesh(mesh.devices.reshape(NZ, NY, NC, NX), ("z", "y", "c", "x"))
    spec = P(("z", "y", "c"), "x")
    return jax.shard_map(
        body, mesh=finer, in_specs=(spec,) * 5, out_specs=(spec,) * 4, check_vma=False
    )
```

time: 92.7 us -> 78.3 us (0.84)
  Pallas kernels: 86.9 us -> 77.6 us
  local copies, waits for them, and re-layouts: 4.95 us -> 0 us
    pallas_call x1 -> x2, Pallas kernels: 86.9 us -> 77.6 us  [the longest x1 75.3 us: body(): pl.pallas_call(kernel, out_shape=shapes, in_specs=[anywhere] * 5, out_spe...]
    unnamed x10 -> x0, local copies, waits for them, and re-layouts: 4.95 us -> none
where the time goes in v2:
time: 78.3 us; the launch traced here: 78.2 us
  Pallas kernels  77.6 us (99%)
    pallas_call x1, Pallas kernels, body(): pl.pallas_call(kernel, out_shape=shapes, in_specs=[anywhere] * 5, out_spe...  75.3 us
    pallas_call x1, Pallas kernels, body(): pl.pallas_call(handed_out, out_shape=shapes, in_specs=[anywhere] * 4, out...  2.31 us

profile of v2, /device:TPU:1, one launch (start us, length us, event | category | flops | bytes accessed | tf_op | source)
XLA Modules:
  0.0 78.2 jit_solution(9911371205099006131)
XLA Ops:
  0.6 75.3 %layer_backward.1 = (bf16[256,1024]{1,0:T(8,128)(2,1)}, bf16[256,1024]{1,0:T(8,128)(2,1)}, bf16[256,1024]{1,0:T(8,128)(2,1)}, f32[48,1024]{1,0:T(8,128)}) custom-call(bf16[256,1024]{1,0:T(8,128)(2,1)} %q_hbm.1, bf16[256,1024]{1,0:T(8,128)(2,1)} %k_hbm.1, bf16[256,1024]{1,0:T(8,128)(2,1)} %v_hbm.1, bf16[48,1024]{1,0:T(8,128)(2,1)} %w_hbm.1, ...), custom_call_target="tpu_custom_call" | custom-call | tf_op jit(solution)/shard_map/layer_backward/pallas_call | solution.py:666
  75.9 2.3 %hand_out.1 = (bf16[256,1024]{1,0:T(8,128)(2,1)}, bf16[256,1024]{1,0:T(8,128)(2,1)}, bf16[256,1024]{1,0:T(8,128)(2,1)}, f32[48,1024]{1,0:T(8,128)}) custom-call(bf16[256,1024]{1,0:T(8,128)(2,1)} %get-tuple-element.8.refs_0_, bf16[256,1024]{1,0:T(8,128)(2,1)} %get-tuple-element.9.refs_1_, bf16[256,1024]{1,0:T(8,128)(2,1)} %get-tuple-element.10.refs_2_, ...), custom_call_target="tpu_custom_call" | custom-call | tf_op jit(solution)/shard_map/hand_out/pallas_call | solution.py:677

commit v3 on v2

--- a/solution.py
+++ b/solution.py
@@ -12,6 +12,7 @@
 BLK = 256
 EPS = 1e-06
 NZ, NY, NC, NX = 8, 4, 2, 4
+CHIPS = NZ * NY
 HEADS = 8
 ROWS = 48
 WIDTH = 1024
@@ -41,10 +42,9 @@
     gq_hbm, gk_hbm, gv_hbm, gw_hbm,
     q, k, v, wb, cot, cot_t, cot_o, normed, scores, raw, inv, da, draw, pk, pv, gq, gk, gv, gw,
     part, st1, r1, st2, r2, red, zst, zr, qst, qr, qy1s, qy1r, qy2s, qy2r,
-    own, s_send, s_recv, a_send, a_recv, a_pre, b_tot, b1_recv, b_base, b2_recv,
-    c_send, c_recv, e_send, e_recv,
+    own, s_send, s_recv, a_send, a_recv, c_send, c_recv, e_send, e_recv,
     load_sem, store_sem, cx1, cx2, zp_sem, yp1, yp2, qy1, qy2, zq, sib, tsib, nsib,
-    ry1, ry2, rz, qz, qya, qyb, ss, sa, sb1, sb2, sc, se,
+    ry1, ry2, rz, qz, qya, qyb, ss, sa, sc, se,
 ):
     z, y, c, x = (lax.axis_index(n) for n in ("z", "y", "c", "x"))
     up_z, dn_z = lax.rem(z + 1, NZ), lax.rem(z + NZ - 1, NZ)
@@ -74,14 +74,84 @@
     for load in loads:
         load.start()
 
-    peers = [{"c": other}]
-    peers += [{"y": lax.rem(y + o, NY)} for o in range(1, NY)]
-    peers += [{"z": lax.rem(z + o, NZ)} for o in range(1, NZ)]
-    peers += list(xdir)
+    chip = z * NY + y
+
+    def chip_peer(o):
+        t = lax.rem(chip + o, CHIPS)
+        return t, {"z": lax.div(t, NY), "y": lax.rem(t, NY)}
+
     barrier = pltpu.get_barrier_semaphore()
-    for peer in peers:
+
+    def greet(peer):
         pl.semaphore_signal(barrier, inc=1, device_id=peer, device_id_type=pl.DeviceIdType.MESH)
-    pl.semaphore_wait(barrier, len(peers))
+
+    @pl.loop(1, CHIPS)
+    def _(o):
+        greet(chip_peer(o)[1])
+
+    for peer in ({"c": other}, *xdir):
+        greet(peer)
+
+    def cols_of(h):
+        return pl.ds(pl.multiple_of(h * HDIM, HDIM), HDIM)
+
+    def for_heads(first, count, fn, unroll=2):
+        @pl.loop(0, count // unroll)
+        def _(i):
+            for u in range(unroll):
+                fn(first + i * unroll + u)
+
+    mask = (
+        lax.broadcasted_iota(jnp.int32, (BLK, BLK), 0)
+        >= lax.broadcasted_iota(jnp.int32, (BLK, BLK), 1)
+    )
+
+    def kv_head(h):
+        cs = cols_of(h)
+        own[0, h] = dot_tn(k[:, cs], v[:, cs])
+
+    def score_head(h):
+        cs = cols_of(h)
+        s = jnp.where(mask, dot_nt(q[:, cs], k[:, cs]), 0.0).astype(BF16)
+        scores[h] = s
+        raw[:, cs] = dot_nn(s, v[:, cs])
+
+    def norm_head(h):
+        cs = cols_of(h)
+        r = raw[:, cs] + dot_nn(q[:, cs], e_recv[0, h])
+        i = lax.rsqrt(jnp.mean(r * r, axis=-1, keepdims=True) + EPS)
+        a = r * i
+        raw[:, cs] = a
+        inv[h] = i
+        normed[0:BLK, cs] = a.astype(BF16)
+
+    def draw_head(h):
+        cs = cols_of(h)
+        d, a = da[:, cs], raw[:, cs]
+        center = jnp.mean(d * a, axis=-1, keepdims=True)
+        dr = (inv[h] * (d - a * center)).astype(BF16)
+        draw[:, cs] = dr
+        own[1, h] = dot_tn(q[:, cs], dr)
+
+    def local_grad_head(h):
+        cs = cols_of(h)
+        dr = draw[:, cs]
+        ds = jnp.where(mask, dot_nt(dr, v[:, cs]), 0.0).astype(BF16)
+        gq[:, cs] = (dot_nn(ds, k[:, cs]) + dot_nt(dr, e_recv[0, h])).astype(BF16)
+        pk[:, cs] = dot_tn(ds, q[:, cs])
+        pv[:, cs] = dot_tn(scores[h], dr)
+
+    def final_grad_head(h):
+        cs = cols_of(h)
+        gk[:, cs] = (pk[:, cs] + dot_nt(v[:, cs], e_recv[1, h])).astype(BF16)
+        gv[:, cs] = (pv[:, cs] + dot_nn(k[:, cs], e_recv[1, h])).astype(BF16)
+
+    for i in (2, 3):
+        loads[i].wait()
+    for_heads(0, 8, kv_head, 4)
+    loads[4].wait()
+    for_heads(0, 8, score_head, 4)
+    pl.semaphore_wait(barrier, CHIPS + 2)
 
     loads[0].wait()
     cot1 = [send(cot.at[x], cot.at[x], cx1, (d,), xdir[d]) for d in (0, 1)]
@@ -175,10 +245,32 @@
         blk = wb.at[ag_z[i], :, c]
         sib_c[i] = send(blk, blk, sib, (i,), {"c": other})
 
-    order = (range(8), range(7, -1, -1))
-    y_order = (range(NY), range(NY - 1, -1, -1))
-    s_c, a_c, b1_c, b2_c, c_c, e_c = {}, {}, {}, {}, {}, {}
+    order = (range(CHIPS), range(CHIPS - 1, -1, -1))
+    s_c, e_c = {}, {}
     mine4, rest4 = pl.ds(c * 4, 4), pl.ds(other * 4, 4)
+    state4 = (4, HDIM, HDIM)
+
+    def spread(src, dst, sem, s):
+        @pl.loop(1, CHIPS)
+        def _(o):
+            t, dev = chip_peer(o)
+            pltpu.make_async_remote_copy(
+                src_ref=src.at[s, t], dst_ref=dst.at[s, chip],
+                send_sem=sem.at[0, s], recv_sem=sem.at[1, s],
+                device_id=dev, device_id_type=pl.DeviceIdType.MESH,
+            ).start()
+
+        dst[s, chip] = src[s, chip]
+        all_but_one = pl.ds(0, CHIPS - 1)
+        whole = pltpu.make_async_remote_copy(
+            src_ref=src.at[s, all_but_one], dst_ref=dst.at[s, all_but_one],
+            send_sem=sem.at[0, s], recv_sem=sem.at[1, s],
+            device_id=chip_peer(1)[1], device_id_type=pl.DeviceIdType.MESH,
+        )
+        pending.append(whole)
+        return whole
+
+    a_c, c_c = {}, {}
 
     def scan_start(s):
         s_send[s] = own[s, rest4].astype(BF16)
@@ -187,53 +279,21 @@
     def scan_a(s):
         s_c[s].wait_recv()
         total = own[s, mine4] + s_recv[s].astype(F32)
-        a_send[s] = total.astype(BF16)
-        for o in range(1, NY):
-            t = lax.rem(y + o, NY)
-            a_c[s, o] = send(a_send.at[s, t], a_recv.at[s, y], sa, (s, o), {"y": t})
-        a_recv[s, y] = a_send[s, y]
-
-    def scan_b1(s):
-        for o in range(1, NY):
-            a_c[s, o].wait_recv()
-        run = jnp.zeros((HDIM, HDIM), F32)
-        for t in y_order[s]:
-            a_pre[s, t] = run
-            run = run + a_recv[s, t].astype(F32)
-        b_tot[s] = run.reshape(NZ, 16, HDIM)
-        for o in range(1, NZ):
-            t = lax.rem(z + o, NZ)
-            b1_c[s, o] = send(b_tot.at[s, t], b1_recv.at[s, z], sb1, (s, o), {"z": t})
-        b1_recv[s, z] = b_tot[s, z]
-
-    def scan_b2(s):
-        for o in range(1, NZ):
-            b1_c[s, o].wait_recv()
+        a_send[s] = total.astype(BF16).reshape(CHIPS, 16, HDIM)
+        a_c[s] = spread(a_send, a_recv, sa, s)
+
+    def scan_c(s):
+        a_c[s].wait_recv()
         run = jnp.zeros((16, HDIM), F32)
         for t in order[s]:
-            b_base[s, t] = run
-            run = run + b1_recv[s, t]
-        for o in range(1, NZ):
-            t = lax.rem(z + o, NZ)
-            b2_c[s, o] = send(b_base.at[s, t], b2_recv.at[s, z], sb2, (s, o), {"z": t})
-        b2_recv[s, z] = b_base[s, z]
-
-    def scan_c(s):
-        for o in range(1, NZ):
-            b2_c[s, o].wait_recv()
-        base = b2_recv[s].reshape(HDIM, HDIM)
-        for t in range(NY):
-            c_send[s, t] = (base + a_pre[s, t]).astype(BF16)
-        for o in range(1, NY):
-            t = lax.rem(y + o, NY)
-            c_c[s, o] = send(c_send.at[s, t], c_recv.at[s, y], sc, (s, o), {"y": t})
-        c_recv[s, y] = c_send[s, y]
+            c_send[s, t] = run.astype(BF16)
+            run = run + a_recv[s, t].astype(F32)
+        c_c[s] = spread(c_send, c_recv, sc, s)
 
     def scan_e(s):
-        for o in range(1, NY):
-            c_c[s, o].wait_recv()
+        c_c[s].wait_recv()
         first = c == s
-        outer = c_recv[s].astype(F32)
+        outer = c_recv[s].reshape(state4).astype(F32)
         after_own = outer + own[s, mine4]
         after_sib = outer + s_recv[s].astype(F32)
         e_send[s] = jnp.where(first, after_own, outer).astype(BF16)
@@ -242,60 +302,6 @@
 
     def scan_end(s):
         e_c[s].wait_recv()
-
-    def cols_of(h):
-        return pl.ds(pl.multiple_of(h * HDIM, HDIM), HDIM)
-
-    def for_heads(first, count, fn, unroll=2):
-        @pl.loop(0, count // unroll)
-        def _(i):
-            for u in range(unroll):
-                fn(first + i * unroll + u)
-
-    mask = (
-        lax.broadcasted_iota(jnp.int32, (BLK, BLK), 0)
-        >= lax.broadcasted_iota(jnp.int32, (BLK, BLK), 1)
-    )
-
-    def kv_head(h):
-        cs = cols_of(h)
-        own[0, h] = dot_tn(k[:, cs], v[:, cs])
-
-    def score_head(h):
-        cs = cols_of(h)
-        s = jnp.where(mask, dot_nt(q[:, cs], k[:, cs]), 0.0).astype(BF16)
-        scores[h] = s
-        raw[:, cs] = dot_nn(s, v[:, cs])
-
-    def norm_head(h):
-        cs = cols_of(h)
-        r = raw[:, cs] + dot_nn(q[:, cs], e_recv[0, h])
-        i = lax.rsqrt(jnp.mean(r * r, axis=-1, keepdims=True) + EPS)
-        a = r * i
-        raw[:, cs] = a
-        inv[h] = i
-        normed[0:BLK, cs] = a.astype(BF16)
-
-    def draw_head(h):
-        cs = cols_of(h)
-        d, a = da[:, cs], raw[:, cs]
-        center = jnp.mean(d * a, axis=-1, keepdims=True)
-        dr = (inv[h] * (d - a * center)).astype(BF16)
-        draw[:, cs] = dr
-        own[1, h] = dot_tn(q[:, cs], dr)
-
-    def local_grad_head(h):
-        cs = cols_of(h)
-        dr = draw[:, cs]
-        ds = jnp.where(mask, dot_nt(dr, v[:, cs]), 0.0).astype(BF16)
-        gq[:, cs] = (dot_nn(ds, k[:, cs]) + dot_nt(dr, e_recv[0, h])).astype(BF16)
-        pk[:, cs] = dot_tn(ds, q[:, cs])
-        pv[:, cs] = dot_tn(scores[h], dr)
-
-    def final_grad_head(h):
-        cs = cols_of(h)
-        gk[:, cs] = (pk[:, cs] + dot_nt(v[:, cs], e_recv[1, h])).astype(BF16)
-        gv[:, cs] = (pv[:, cs] + dot_nn(k[:, cs], e_recv[1, h])).astype(BF16)
 
     x_order = (x, dn_x, up_x, far_x)
     tsib_c = {}
@@ -449,16 +455,6 @@
     half8 = ((0, 4), (4, 4))
     nsib_c = []
 
-    def kv():
-        loads[2].wait()
-        loads[3].wait()
-        for_heads(0, 8, kv_head, 4)
-
-    def score(n):
-        if n == 0:
-            loads[4].wait()
-        for_heads(*half8[n], score_head, 4)
-
     def norm(n):
         for_heads(*half8[n], norm_head, 4)
         blk = pl.ds(512 * n, 512)
@@ -487,118 +483,111 @@
 
     loads[1].wait()
     ag_start()
-    kv()
     scan_start(0)
-    score(0)
-    score(1)
+    turn(0)
     scan_a(0)
     ag_q1()
-    forward_yp(0)
     ag_p(1)
     send_zq(0, 1)
-    turn(0)
+    forward_yp(0)
+    ag_q2()
+    forward_yp(1)
     send_zq(1, 1)
-    ag_q2()
     send_zq(2, 1)
-    scan_b1(0)
+    forward_yp(2)
     send_sib(0)
     ag_p(2)
+    scan_c(0)
     cot_forward()
-    forward_yp(1)
     send_zq(0, 2)
+    turn(2)
+    send_zq(3, 1)
+    send_zq(1, 2)
+    send_sib(1)
+    send_sib(2)
     turn(1)
-    forward_yp(2)
-    send_zq(1, 2)
-    send_zq(3, 1)
-    turn(2)
     send_zq(2, 2)
     forward_yp(3)
-    scan_b2(0)
+    ag_p(3)
     forward_yp(4)
-    ag_p(3)
+    cot_wait()
+    d_attn((0, 1, 2), True)
+    send_zq(3, 2)
+    send_sib(3)
     send_zq(0, 3)
-    send_sib(1)
-    send_sib(2)
     send_zq(1, 3)
-    cot_wait()
+    forward_yp(5)
+    scan_e(0)
+    forward_yp(6)
+    send_zq(2, 3)
+    ag_p(4)
+    send_sib(4)
     turn(3)
-    send_zq(3, 2)
-    send_zq(2, 3)
-    send_sib(3)
-    send_sib(4)
-    d_attn((0, 1, 2), True)
-    scan_c(0)
-    forward_yp(5)
-    forward_yp(6)
-    ag_p(4)
-    send_zq(3, 3)
-    d_attn((3, 4))
-    send_sib(5)
-    scan_e(0)
-    send_sib(6)
-    forward_yp(7)
     scan_end(0)
     norm(0)
+    send_zq(3, 3)
     norm(1)
-    d_attn((5, 6))
-    send_sib(7)
+    send_sib(6)
+    send_sib(5)
+    d_attn((3, 4))
+    forward_yp(7)
     sib_wait()
     product(0, 1)
     qchain(0, 0)
+    step1(0)
     qchain(1, 0)
-    step1(0)
     product(1, 3)
+    step1(2)
+    step1(1)
+    d_attn((5, 6))
+    send_sib(7)
+    step2(0)
+    qchain(0, 1)
+    qchain(1, 1)
+    product(3, 5)
     d_attn((7,))
     for_heads(0, 8, draw_head, 4)
     scan_start(1)
-    qchain(0, 1)
-    qchain(1, 1)
-    step2(0)
-    step1(1)
-    step1(2)
-    scan_a(1)
-    product(3, 5)
-    step1(3)
     step1(4)
-    product(5, 8)
+    qchain(0, 2)
+    step2(1)
     step3(0)
     chain(0)
-    qchain(0, 2)
+    step2(2)
+    scan_a(1)
+    step1(3)
     qchain(1, 2)
-    step2(1)
-    step2(2)
+    product(5, 8)
+    step1(6)
+    step2(4)
     step1(5)
-    step1(6)
+    step3(1)
     step1(7)
+    qchain(0, 3)
     local_grad(0)
-    scan_b1(1)
-    step2(3)
-    step2(4)
-    qchain(0, 3)
-    step3(1)
-    local_grad(1)
     step3(2)
     chain(1)
+    local_grad(1)
+    step2(3)
+    step2(6)
     qchain(1, 3)
+    step3(4)
+    q_y1()
+    scan_c(1)
     step2(5)
-    step2(6)
     step2(7)
-    scan_b2(1)
-    q_y1()
     step3(3)
-    step3(4)
     chain(2)
+    step3(6)
+    q_y2()
     step3(5)
-    step3(6)
-    scan_c(1)
     chain(3)
     step3(7)
-    q_y2()
-    chain_end()
+    scan_e(1)
     q_end()
-    scan_e(1)
     scan_end(1)
     final_grad()
+    chain_end()
     store(3, gw, gw_hbm)
     for copy in stores:
         copy.wait()
@@ -647,10 +636,8 @@
         vm((2, PA, WIDTH), BF16), vm((2, PA, WIDTH), BF16),
         vm((2, HEADS, *state), F32),
         vm((2, 4, *state), BF16), vm((2, 4, *state), BF16),
-        vm((2, 4, *state), BF16), vm((2, 4, *state), BF16), vm((2, 4, *state), F32),
-        vm((2, NZ, 16, HDIM), F32), vm((2, NZ, 16, HDIM), F32),
-        vm((2, NZ, 16, HDIM), F32), vm((2, NZ, 16, HDIM), F32),
-        vm((2, 4, *state), BF16), vm((2, 4, *state), BF16),
+        vm((2, CHIPS, 16, HDIM), BF16), vm((2, CHIPS, 16, HDIM), BF16),
+        vm((2, CHIPS, 16, HDIM), BF16), vm((2, CHIPS, 16, HDIM), BF16),
         vm((2, 4, *state), BF16), vm((2, HEADS, *state), BF16),
         dma((5,)), dma((4,)), dma((2, 2)), dma((2, 2)),
         dma((2, 2, 4)), dma((2, 2, 8)), dma((2, 2, 8)),
@@ -658,7 +645,7 @@
         dma((2, 8)), dma((2, 4, 2)), dma((2, 2)),
         dma((2, 2, 8)), dma((2, 2, 8)), dma((2, 2, 4)), dma((2, 2, 2, 4)),
         dma((2, 2)), dma((2, 2)),
-        dma((2, 2)), dma((2, 2, 4)), dma((2, 2, 8)), dma((2, 2, 8)), dma((2, 2, 4)), dma((2, 2)),
+        dma((2, 2)), dma((2, 2)), dma((2, 2)), dma((2, 2)),
     ]
     grad = jax.ShapeDtypeStruct((BLK, WIDTH), BF16)
     shapes = (grad, grad, grad, jax.ShapeDtypeStruct((ROWS, WIDTH), F32))

time: 78.3 us -> 72.9 us (0.931)
  Pallas kernels: 77.6 us -> 72.2 us
    pallas_call x1, Pallas kernels: 75.3 us -> 69.9 us  [body(): pl.pallas_call(kernel, out_shape=shapes, in_specs=[anywhere] * 5, out_spe...]
where the time goes in v3:
time: 72.9 us; the launch traced here: 72.8 us
  Pallas kernels  72.2 us (99%)
    pallas_call x1, Pallas kernels, body(): pl.pallas_call(kernel, out_shape=shapes, in_specs=[anywhere] * 5, out_spe...  69.9 us
    pallas_call x1, Pallas kernels, body(): pl.pallas_call(handed_out, out_shape=shapes, in_specs=[anywhere] * 4, out...  2.31 us

profile of v3, /device:TPU:1, one launch (start us, length us, event | category | flops | bytes accessed | tf_op | source)
XLA Modules:
  0.0 72.8 jit_solution(10551319409594326518)
XLA Ops:
  0.6 69.9 %layer_backward.1 = (bf16[256,1024]{1,0:T(8,128)(2,1)}, bf16[256,1024]{1,0:T(8,128)(2,1)}, bf16[256,1024]{1,0:T(8,128)(2,1)}, f32[48,1024]{1,0:T(8,128)}) custom-call(bf16[256,1024]{1,0:T(8,128)(2,1)} %q_hbm.1, bf16[256,1024]{1,0:T(8,128)(2,1)} %k_hbm.1, bf16[256,1024]{1,0:T(8,128)(2,1)} %v_hbm.1, bf16[48,1024]{1,0:T(8,128)(2,1)} %w_hbm.1, ...), custom_call_target="tpu_custom_call" | custom-call | tf_op jit(solution)/shard_map/layer_backward/pallas_call | solution.py:653
  70.5 2.3 %hand_out.1 = (bf16[256,1024]{1,0:T(8,128)(2,1)}, bf16[256,1024]{1,0:T(8,128)(2,1)}, bf16[256,1024]{1,0:T(8,128)(2,1)}, f32[48,1024]{1,0:T(8,128)}) custom-call(bf16[256,1024]{1,0:T(8,128)(2,1)} %get-tuple-element.8.refs_0_, bf16[256,1024]{1,0:T(8,128)(2,1)} %get-tuple-element.9.refs_1_, bf16[256,1024]{1,0:T(8,128)(2,1)} %get-tuple-element.10.refs_2_, ...), custom_call_target="tpu_custom_call" | custom-call | tf_op jit(solution)/shard_map/hand_out/pallas_call | solution.py:664

commit v4 on v3

--- a/solution.py
+++ b/solution.py
@@ -39,11 +39,11 @@
 
 def kernel(
     q_hbm, k_hbm, v_hbm, w_hbm, cot_hbm,
-    gq_hbm, gk_hbm, gv_hbm, gw_hbm,
-    q, k, v, wb, cot, cot_t, cot_o, normed, scores, raw, inv, da, draw, pk, pv, gq, gk, gv, gw,
+    gq, gk, gv, gw,
+    q, k, v, wb, cot, cot_t, cot_o, normed, scores, raw, inv, da, draw, pk, pv,
     part, st1, r1, st2, r2, red, zst, zr, qst, qr, qy1s, qy1r, qy2s, qy2r,
     own, s_send, s_recv, a_send, a_recv, c_send, c_recv, e_send, e_recv,
-    load_sem, store_sem, cx1, cx2, zp_sem, yp1, yp2, qy1, qy2, zq, sib, tsib, nsib,
+    line_sem, load_sem, cx1, cx2, zp_sem, yp1, yp2, qy1, qy2, zq, sib, tsib, nsib,
     ry1, ry2, rz, qz, qya, qyb, ss, sa, sc, se,
 ):
     z, y, c, x = (lax.axis_index(n) for n in ("z", "y", "c", "x"))
@@ -85,11 +85,10 @@
     def greet(peer):
         pl.semaphore_signal(barrier, inc=1, device_id=peer, device_id_type=pl.DeviceIdType.MESH)
 
-    @pl.loop(1, CHIPS)
-    def _(o):
-        greet(chip_peer(o)[1])
-
-    for peer in ({"c": other}, *xdir):
+    near = [{"c": other}, *xdir]
+    near += [{"y": lax.rem(y + o, NY)} for o in range(1, NY)]
+    near += [{"z": lax.rem(z + o, NZ)} for o in range(1, NZ)]
+    for peer in near:
         greet(peer)
 
     def cols_of(h):
@@ -151,7 +150,10 @@
     for_heads(0, 8, kv_head, 4)
     loads[4].wait()
     for_heads(0, 8, score_head, 4)
-    pl.semaphore_wait(barrier, CHIPS + 2)
+    pl.semaphore_wait(barrier, len(near))
+    for o in range(1, NY):
+        dev = {"y": lax.rem(y + o, NY)}
+        pl.semaphore_signal(line_sem, inc=1, device_id=dev, device_id_type=pl.DeviceIdType.MESH)
 
     loads[0].wait()
     cot1 = [send(cot.at[x], cot.at[x], cx1, (d,), xdir[d]) for d in (0, 1)]
@@ -280,6 +282,8 @@
         s_c[s].wait_recv()
         total = own[s, mine4] + s_recv[s].astype(F32)
         a_send[s] = total.astype(BF16).reshape(CHIPS, 16, HDIM)
+        if s == 0:
+            pl.semaphore_wait(line_sem, NY - 1)
         a_c[s] = spread(a_send, a_recv, sa, s)
 
     def scan_c(s):
@@ -445,13 +449,6 @@
         total = part[7, 3, PB:ROWS] + (qy2r[0].astype(F32) + qy2r[1].astype(F32))
         gw[PB:ROWS] = total * GRADW_SCALE
 
-    stores = []
-
-    def store(i, src_ref, dst_ref):
-        copy = pltpu.make_async_copy(src_ref, dst_ref, store_sem.at[i])
-        copy.start()
-        stores.append(copy)
-
     half8 = ((0, 4), (4, 4))
     nsib_c = []
 
@@ -473,13 +470,9 @@
 
     def local_grad(n):
         for_heads(*half8[n], local_grad_head, 4)
-        if n == 1:
-            store(0, gq, gq_hbm)
 
     def final_grad():
         for_heads(0, 8, final_grad_head, 4)
-        store(1, gk, gk_hbm)
-        store(2, gv, gv_hbm)
 
     loads[1].wait()
     ag_start()
@@ -495,116 +488,109 @@
     send_zq(1, 1)
     send_zq(2, 1)
     forward_yp(2)
+    scan_c(0)
     send_sib(0)
     ag_p(2)
-    scan_c(0)
     cot_forward()
     send_zq(0, 2)
     turn(2)
     send_zq(3, 1)
+    send_sib(1)
+    turn(1)
     send_zq(1, 2)
-    send_sib(1)
     send_sib(2)
-    turn(1)
     send_zq(2, 2)
     forward_yp(3)
+    forward_yp(4)
     ag_p(3)
-    forward_yp(4)
     cot_wait()
     d_attn((0, 1, 2), True)
     send_zq(3, 2)
+    scan_e(0)
+    send_zq(2, 3)
+    send_sib(4)
+    send_zq(0, 3)
     send_sib(3)
-    send_zq(0, 3)
+    ag_p(4)
     send_zq(1, 3)
     forward_yp(5)
-    scan_e(0)
-    forward_yp(6)
-    send_zq(2, 3)
-    ag_p(4)
-    send_sib(4)
-    turn(3)
     scan_end(0)
     norm(0)
+    norm(1)
+    turn(3)
+    forward_yp(6)
     send_zq(3, 3)
-    norm(1)
-    send_sib(6)
-    send_sib(5)
     d_attn((3, 4))
     forward_yp(7)
     sib_wait()
     product(0, 1)
+    send_sib(5)
+    step1(0)
     qchain(0, 0)
-    step1(0)
+    send_sib(6)
     qchain(1, 0)
     product(1, 3)
+    send_sib(7)
+    step1(1)
     step1(2)
-    step1(1)
+    product(3, 5)
+    qchain(0, 1)
+    step1(4)
+    qchain(1, 1)
+    step2(0)
     d_attn((5, 6))
-    send_sib(7)
-    step2(0)
-    qchain(0, 1)
-    qchain(1, 1)
-    product(3, 5)
     d_attn((7,))
     for_heads(0, 8, draw_head, 4)
     scan_start(1)
-    step1(4)
     qchain(0, 2)
+    step1(3)
     step2(1)
+    step2(2)
     step3(0)
     chain(0)
-    step2(2)
     scan_a(1)
-    step1(3)
     qchain(1, 2)
     product(5, 8)
+    qchain(0, 3)
+    step1(5)
+    step2(3)
     step1(6)
-    step2(4)
-    step1(5)
     step3(1)
     step1(7)
-    qchain(0, 3)
+    step2(4)
     local_grad(0)
     step3(2)
     chain(1)
     local_grad(1)
-    step2(3)
+    step2(5)
+    qchain(1, 3)
+    step3(3)
+    scan_c(1)
+    q_y1()
     step2(6)
-    qchain(1, 3)
+    step2(7)
     step3(4)
-    q_y1()
-    scan_c(1)
-    step2(5)
-    step2(7)
-    step3(3)
     chain(2)
+    step3(5)
+    q_y2()
     step3(6)
-    q_y2()
-    step3(5)
     chain(3)
+    scan_e(1)
     step3(7)
-    scan_e(1)
     q_end()
     scan_end(1)
     final_grad()
     chain_end()
-    store(3, gw, gw_hbm)
-    for copy in stores:
-        copy.wait()
     for copy in pending:
         copy.wait_send()
 
 
 def handed_out(*refs):
-    ins, outs, held, sems = refs[:4], refs[4:8], refs[8:12], refs[12]
-    into = [pltpu.make_async_copy(a, b, sems.at[0, i]) for i, (a, b) in enumerate(zip(ins, held))]
-    back = [pltpu.make_async_copy(a, b, sems.at[1, i]) for i, (a, b) in enumerate(zip(held, outs))]
-    for copy in into:
+    ins, outs, sems = refs[:4], refs[4:8], refs[8]
+    copies = [pltpu.make_async_copy(a, b, sems.at[i]) for i, (a, b) in enumerate(zip(ins, outs))]
+    for copy in copies:
         copy.start()
-    for i in range(4):
-        into[i].wait()
-        back[i].start()
-    for copy in back:
+    for copy in copies:
         copy.wait()
 
 
@@ -624,8 +610,6 @@
         vm((BLK, WIDTH), F32),
         vm((BLK, WIDTH), BF16),
         vm((BLK, WIDTH), F32), vm((BLK, WIDTH), F32),
-        vm((BLK, WIDTH), BF16), vm((BLK, WIDTH), BF16), vm((BLK, WIDTH), BF16),
-        vm((ROWS, WIDTH), F32),
         vm((NZ, NY, ROWS, WIDTH), F32),
         vm((8, PB, WIDTH), BF16), vm((2, 8, PA, WIDTH), BF16),
         vm((2, 8, PB, WIDTH), BF16), vm((2, 8, PB, WIDTH), BF16),
@@ -639,7 +623,8 @@
         vm((2, CHIPS, 16, HDIM), BF16), vm((2, CHIPS, 16, HDIM), BF16),
         vm((2, CHIPS, 16, HDIM), BF16), vm((2, CHIPS, 16, HDIM), BF16),
         vm((2, 4, *state), BF16), vm((2, HEADS, *state), BF16),
-        dma((5,)), dma((4,)), dma((2, 2)), dma((2, 2)),
+        pltpu.SemaphoreType.REGULAR,
+        dma((5,)), dma((2, 2)), dma((2, 2)),
         dma((2, 2, 4)), dma((2, 2, 8)), dma((2, 2, 8)),
         dma((2, 2)), dma((2, 2)), dma((2, 4, 2, 4)),
         dma((2, 8)), dma((2, 4, 2)), dma((2, 2)),
@@ -649,24 +634,30 @@
     ]
     grad = jax.ShapeDtypeStruct((BLK, WIDTH), BF16)
     shapes = (grad, grad, grad, jax.ShapeDtypeStruct((ROWS, WIDTH), F32))
-    anywhere = pl.BlockSpec(memory_space=pl.ANY)
+    far = pl.BlockSpec(memory_space=pltpu.HBM)
+    close = pl.BlockSpec(memory_space=pltpu.VMEM)
+    ins = [
+        pltpu.with_memory_space_constraint(a, pltpu.HBM)
+        for a in (query_act, key_act, value_act, out_weight, out_cotangent)
+    ]
     made = pl.pallas_call(
         kernel,
         out_shape=shapes,
-        in_specs=[anywhere] * 5,
-        out_specs=[anywhere] * 4,
+        in_specs=[far] * 5,
+        out_specs=[close] * 4,
         scratch_shapes=scratch,
         compiler_params=pltpu.CompilerParams(
-            collective_id=0, has_side_effects=True, vmem_limit_bytes=56 * 1024 * 1024
+            collective_id=0, has_side_effects=True, vmem_limit_bytes=48 * 1024 * 1024
         ),
         name="layer_backward",
-    )(query_act, key_act, value_act, out_weight, out_cotangent)
+    )(*ins)
     return pl.pallas_call(
         handed_out,
         out_shape=shapes,
-        in_specs=[anywhere] * 4,
-        out_specs=[anywhere] * 4,
-        scratch_shapes=[*(vm(s.shape, s.dtype) for s in shapes), dma((2, 4))],
+        in_specs=[close] * 4,
+        out_specs=[far] * 4,
+        scratch_shapes=[dma((4,))],
+        compiler_params=pltpu.CompilerParams(vmem_limit_bytes=4 * 1024 * 1024),
         name="hand_out",
     )(*made)
 

time: 72.9 us -> 69.3 us (0.951)
  Pallas kernels: 72.2 us -> 68.6 us
    pallas_call x2, Pallas kernels: 72.2 us -> 68.6 us  [the longest x1 67.4 us: body(): pl.pallas_call(kernel, out_shape=shapes, in_specs=[far] * 5, out_specs=[c...]
where the time goes in v4:
time: 69.3 us; the launch traced here: 69.2 us
  Pallas kernels  68.6 us (99%)
    pallas_call x1, Pallas kernels, body(): pl.pallas_call(kernel, out_shape=shapes, in_specs=[far] * 5, out_specs=[c...  67.4 us

profile of v4, /device:TPU:1, one launch (start us, length us, event | category | flops | bytes accessed | tf_op | source)
XLA Modules:
  0.0 69.2 jit_solution(15014350770616791101)
XLA Ops:
  0.6 67.4 %layer_backward.1 = (bf16[256,1024]{1,0:T(8,128)(2,1)S(1)}, bf16[256,1024]{1,0:T(8,128)(2,1)S(1)}, bf16[256,1024]{1,0:T(8,128)(2,1)S(1)}, f32[48,1024]{1,0:T(8,128)S(1)}) custom-call(bf16[256,1024]{1,0:T(8,128)(2,1)} %q_hbm.1, bf16[256,1024]{1,0:T(8,128)(2,1)} %k_hbm.1, bf16[256,1024]{1,0:T(8,128)(2,1)} %v_hbm.1, bf16[48,1024]{1,0:T(8,128)(2,1)} %w_hbm.1, ...), custom_call_target="tpu_custom_call" | custom-call | tf_op jit(solution)/shard_map/layer_backward/pallas_call | solution.py:643
  68.0 1.2 %hand_out.1 = (bf16[256,1024]{1,0:T(8,128)(2,1)}, bf16[256,1024]{1,0:T(8,128)(2,1)}, bf16[256,1024]{1,0:T(8,128)(2,1)}, f32[48,1024]{1,0:T(8,128)}) custom-call(bf16[256,1024]{1,0:T(8,128)(2,1)S(1)} %get-tuple-element.8.refs_0_, bf16[256,1024]{1,0:T(8,128)(2,1)S(1)} %get-tuple-element.9.refs_1_, bf16[256,1024]{1,0:T(8,128)(2,1)S(1)} %get-tuple-element.10.refs_2_, ...), custom_call_target="tpu_custom_call" | custom-call | tf_op jit(solution)/shard_map/hand_out/pallas_call | solution.py:654

commit v5 on v4

--- a/solution.py
+++ b/solution.py
@@ -147,9 +147,9 @@
 
     for i in (2, 3):
         loads[i].wait()
-    for_heads(0, 8, kv_head, 4)
+    for_heads(0, 8, kv_head, 8)
     loads[4].wait()
-    for_heads(0, 8, score_head, 4)
+    for_heads(0, 8, score_head, 8)
     pl.semaphore_wait(barrier, len(near))
     for o in range(1, NY):
         dev = {"y": lax.rem(y + o, NY)}
@@ -331,17 +331,14 @@
         for i in idx:
             sib_c[i].wait_recv()
 
-        @pl.loop(0, 4)
-        def _(n):
-            cs = pl.ds(pl.multiple_of(n * 256, 256), 256)
-            lhs, rhs = [], []
-            for i in idx:
-                zo = ag_z[i]
-                lanes = pl.ds(pl.multiple_of(lax.rem(zo, 2) * SLAB, 128), SLAB)
-                lhs.append(cot[lax.div(zo, 2), :, lanes])
-                rhs.append(wb[zo, :, :, :, cs].reshape(SLAB, 256))
-            t = dot_nn(jnp.concatenate(lhs, 1), jnp.concatenate(rhs, 0))
-            da[:, cs] = t if first else da[:, cs] + t
+        lhs, rhs = [], []
+        for i in idx:
+            zo = ag_z[i]
+            lanes = pl.ds(pl.multiple_of(lax.rem(zo, 2) * SLAB, 128), SLAB)
+            lhs.append(cot[lax.div(zo, 2), :, lanes])
+            rhs.append(wb[zo].reshape(SLAB, WIDTH))
+        t = dot_nn(jnp.concatenate(lhs, 1), jnp.concatenate(rhs, 0))
+        da[...] = t if first else da[...] + t
 
     up_of, dn_of = (0, 1, 3, 5), (0, 2, 4, 6)
     y_of = (1, 2)
@@ -350,11 +347,8 @@
     def product(lo, hi):
         n = hi - lo
 
-        @pl.loop(0, 4)
-        def _(col):
-            cs = pl.ds(pl.multiple_of(col * 256, 256), 256)
-            acc = dot_nn(cot_t[lo:hi].reshape(n * NY * ROWS, 2 * BLK), normed[:, cs])
-            part[lo:hi, :, :, cs] = acc.reshape(n, NY, ROWS, 256)
+        acc = dot_nn(cot_t[lo:hi].reshape(n * NY * ROWS, 2 * BLK), normed[...])
+        part[lo:hi] = acc.reshape(n, NY, ROWS, WIDTH)
 
     def step1(i):
         st1[i] = part[i, 0, 0:PB].astype(BF16)
@@ -472,7 +466,7 @@
         for_heads(*half8[n], local_grad_head, 4)
 
     def final_grad():
-        for_heads(0, 8, final_grad_head, 4)
+        for_heads(0, 8, final_grad_head, 8)
 
     loads[1].wait()
     ag_start()
@@ -492,91 +486,91 @@
     send_sib(0)
     ag_p(2)
     cot_forward()
-    send_zq(0, 2)
-    turn(2)
+    turn(1)
     send_zq(3, 1)
     send_sib(1)
-    turn(1)
+    turn(2)
+    send_sib(2)
     send_zq(1, 2)
-    send_sib(2)
     send_zq(2, 2)
+    send_zq(0, 2)
     forward_yp(3)
     forward_yp(4)
     ag_p(3)
     cot_wait()
     d_attn((0, 1, 2), True)
+    scan_e(0)
+    send_zq(1, 3)
     send_zq(3, 2)
-    scan_e(0)
-    send_zq(2, 3)
-    send_sib(4)
+    send_sib(3)
+    turn(3)
     send_zq(0, 3)
-    send_sib(3)
-    ag_p(4)
-    send_zq(1, 3)
-    forward_yp(5)
     scan_end(0)
     norm(0)
+    ag_p(4)
     norm(1)
-    turn(3)
+    forward_yp(5)
+    send_sib(4)
+    send_zq(2, 3)
+    send_zq(3, 3)
     forward_yp(6)
-    send_zq(3, 3)
+    sib_wait()
+    product(0, 1)
+    step1(0)
+    qchain(0, 0)
+    qchain(1, 0)
     d_attn((3, 4))
     forward_yp(7)
-    sib_wait()
-    product(0, 1)
+    product(1, 3)
     send_sib(5)
-    step1(0)
-    qchain(0, 0)
+    step1(2)
+    step1(1)
     send_sib(6)
-    qchain(1, 0)
-    product(1, 3)
+    product(3, 5)
+    step2(0)
+    qchain(0, 1)
+    step1(3)
+    step1(4)
     send_sib(7)
-    step1(1)
-    step1(2)
-    product(3, 5)
-    qchain(0, 1)
-    step1(4)
     qchain(1, 1)
-    step2(0)
+    product(5, 8)
+    step2(2)
+    step1(6)
     d_attn((5, 6))
     d_attn((7,))
-    for_heads(0, 8, draw_head, 4)
+    for_heads(0, 8, draw_head, 8)
     scan_start(1)
     qchain(0, 2)
-    step1(3)
-    step2(1)
-    step2(2)
     step3(0)
     chain(0)
+    step2(1)
+    step2(4)
     scan_a(1)
     qchain(1, 2)
-    product(5, 8)
+    step2(3)
+    step3(2)
+    step1(5)
+    local_grad(0)
+    local_grad(1)
     qchain(0, 3)
-    step1(5)
-    step2(3)
-    step1(6)
     step3(1)
+    chain(1)
+    step2(6)
     step1(7)
-    step2(4)
-    local_grad(0)
-    step3(2)
-    chain(1)
-    local_grad(1)
-    step2(5)
+    step3(4)
     qchain(1, 3)
     step3(3)
+    step2(5)
     scan_c(1)
     q_y1()
-    step2(6)
+    step3(6)
+    chain(2)
     step2(7)
-    step3(4)
-    chain(2)
     step3(5)
     q_y2()
-    step3(6)
+    step3(7)
     chain(3)
     scan_e(1)
-    step3(7)
     q_end()
     scan_end(1)
     final_grad()

time: 69.3 us -> 65.9 us (0.951)
  Pallas kernels: 68.6 us -> 64.5 us
    pallas_call x1, Pallas kernels: 67.4 us -> 63.3 us  [body(): pl.pallas_call(kernel, out_shape=shapes, in_specs=[far] * 5, out_specs=[c...]
where the time goes in v5:
time: 65.9 us; the launch traced here: 65.1 us
  Pallas kernels  64.5 us (98%)
    pallas_call x1, Pallas kernels, body(): pl.pallas_call(kernel, out_shape=shapes, in_specs=[far] * 5, out_specs=[c...  63.3 us

profile of v5, /device:TPU:1, one launch (start us, length us, event | category | flops | bytes accessed | tf_op | source)
XLA Modules:
  0.0 65.1 jit_solution(15428966058383393497)
XLA Ops:
  0.6 63.3 %layer_backward.1 = (bf16[256,1024]{1,0:T(8,128)(2,1)S(1)}, bf16[256,1024]{1,0:T(8,128)(2,1)S(1)}, bf16[256,1024]{1,0:T(8,128)(2,1)S(1)}, f32[48,1024]{1,0:T(8,128)S(1)}) custom-call(bf16[256,1024]{1,0:T(8,128)(2,1)} %q_hbm.1, bf16[256,1024]{1,0:T(8,128)(2,1)} %k_hbm.1, bf16[256,1024]{1,0:T(8,128)(2,1)} %v_hbm.1, bf16[48,1024]{1,0:T(8,128)(2,1)} %w_hbm.1, ...), custom_call_target="tpu_custom_call" | custom-call | tf_op jit(solution)/shard_map/layer_backward/pallas_call | solution.py:637
  63.9 1.2 %hand_out.1 = (bf16[256,1024]{1,0:T(8,128)(2,1)}, bf16[256,1024]{1,0:T(8,128)(2,1)}, bf16[256,1024]{1,0:T(8,128)(2,1)}, f32[48,1024]{1,0:T(8,128)}) custom-call(bf16[256,1024]{1,0:T(8,128)(2,1)S(1)} %get-tuple-element.8.refs_0_, bf16[256,1024]{1,0:T(8,128)(2,1)S(1)} %get-tuple-element.9.refs_1_, bf16[256,1024]{1,0:T(8,128)(2,1)S(1)} %get-tuple-element.10.refs_2_, ...), custom_call_target="tpu_custom_call" | custom-call | tf_op jit(solution)/shard_map/hand_out/pallas_call | solution.py:648

commit v6 on v5

--- a/solution.py
+++ b/solution.py
@@ -447,8 +447,9 @@
     nsib_c = []
 
     def norm(n):
-        for_heads(*half8[n], norm_head, 4)
-        blk = pl.ds(512 * n, 512)
+        part8 = (c, other)[n]
+        for_heads(part8 * 4, 4, norm_head, 4)
+        blk = pl.ds(pl.multiple_of(part8 * 512, 512), 512)
         src, dst = normed.at[pl.ds(0, BLK), blk], normed.at[pl.ds(BLK, BLK), blk]
         nsib_c.append(send(src, dst, nsib, (n,), {"c": other}))
 
@@ -465,8 +466,8 @@
     def local_grad(n):
         for_heads(*half8[n], local_grad_head, 4)
 
-    def final_grad():
-        for_heads(0, 8, final_grad_head, 8)
+    def final_grad(n):
+        for_heads((c, other)[n] * 4, 4, final_grad_head, 4)
 
     loads[1].wait()
     ag_start()
@@ -500,13 +501,13 @@
     cot_wait()
     d_attn((0, 1, 2), True)
     scan_e(0)
+    norm(0)
     send_zq(1, 3)
     send_zq(3, 2)
     send_sib(3)
     turn(3)
     send_zq(0, 3)
     scan_end(0)
-    norm(0)
     ag_p(4)
     norm(1)
     forward_yp(5)
@@ -571,9 +572,10 @@
     step3(7)
     chain(3)
     scan_e(1)
+    final_grad(0)
     q_end()
     scan_end(1)
-    final_grad()
+    final_grad(1)
     chain_end()
     for copy in pending:
         copy.wait_send()

time: 65.9 us -> 65.6 us (level)
  no operation moved by 1% of the time
where the time goes in v6:
time: 65.6 us; the launch traced here: 65 us
  Pallas kernels  64.4 us (98%)
    pallas_call x1, Pallas kernels, body(): pl.pallas_call(kernel, out_shape=shapes, in_specs=[far] * 5, out_specs=[c...  63.1 us

profile of v6, /device:TPU:1, one launch (start us, length us, event | category | flops | bytes accessed | tf_op | source)
XLA Modules:
  0.0 65.0 jit_solution(16373139644175308194)
XLA Ops:
  0.6 63.1 %layer_backward.1 = (bf16[256,1024]{1,0:T(8,128)(2,1)S(1)}, bf16[256,1024]{1,0:T(8,128)(2,1)S(1)}, bf16[256,1024]{1,0:T(8,128)(2,1)S(1)}, f32[48,1024]{1,0:T(8,128)S(1)}) custom-call(bf16[256,1024]{1,0:T(8,128)(2,1)} %q_hbm.1, bf16[256,1024]{1,0:T(8,128)(2,1)} %k_hbm.1, bf16[256,1024]{1,0:T(8,128)(2,1)} %v_hbm.1, bf16[48,1024]{1,0:T(8,128)(2,1)} %w_hbm.1, ...), custom_call_target="tpu_custom_call" | custom-call | tf_op jit(solution)/shard_map/layer_backward/pallas_call | solution.py:639
  63.8 1.2 %hand_out.1 = (bf16[256,1024]{1,0:T(8,128)(2,1)}, bf16[256,1024]{1,0:T(8,128)(2,1)}, bf16[256,1024]{1,0:T(8,128)(2,1)}, f32[48,1024]{1,0:T(8,128)}) custom-call(bf16[256,1024]{1,0:T(8,128)(2,1)S(1)} %get-tuple-element.8.refs_0_, bf16[256,1024]{1,0:T(8,128)(2,1)S(1)} %get-tuple-element.9.refs_1_, bf16[256,1024]{1,0:T(8,128)(2,1)S(1)} %get-tuple-element.10.refs_2_, ...), custom_call_target="tpu_custom_call" | custom-call | tf_op jit(solution)/shard_map/hand_out/pallas_call | solution.py:650
